TPU v7x, 256 devices: a whole 4x4x8 slice. The times are simulated.
256 devices in a mesh: expert: 8 (over y, core), dp: 32 (over x, z).
Axes of the slice: x: 4, y: 4, z: 8, core: 2. Of those that a mesh axis runs over, the one named last changes fastest.
Arguments:
- query_act: bfloat16 [512, 64, 1664], P('dp', 'expert'), may hold values from -5 to 5
- key_act: bfloat16 [512, 64, 1664], P('dp', 'expert'), may hold values from -5 to 5
- value_act: bfloat16 [512, 64, 1664], P('dp', 'expert'), may hold values from -6 to 6
- stream: bfloat16 [512, 64, 1664], P('dp', 'expert'), may hold values from -6 to 6
- grad_out: bfloat16 [512, 64, 1664], P('dp', 'expert'), may hold values from -6 to 6
- norm_gain: float32 [1664], replicated, may hold values from 0.25 to 1.75
- route_ids: int32 [32, 8, 128, 1], P('dp', 'expert'), may hold values from 0 to 31; in each aligned block of 128 rows (0 to 127, 128 to 255, ..., all dimensions but the last counted through in order) at most 6 rows name the same one
- gate_prob: float32 [32, 8, 128], P('dp', 'expert'), may hold values from 0.2 to 1
- weight_in: bfloat16 [32, 1664, 4096], P('dp', None, 'expert'), may hold values from -0.15625 to 0.15625
- weight_out: bfloat16 [32, 4096, 1664], P('dp', 'expert'), may hold values from -0.09375 to 0.09375
Outputs:
- grad_query: bfloat16 [512, 64, 1664], P('dp', 'expert')
- grad_key: bfloat16 [512, 64, 1664], P('dp', 'expert')
- grad_value: bfloat16 [512, 64, 1664], P('dp', 'expert')
- grad_stream: bfloat16 [512, 64, 1664], P('dp', 'expert')
- grad_weight_in: bfloat16 [32, 1664, 4096], P('dp', None, 'expert')
- grad_weight_out: bfloat16 [32, 4096, 1664], P('dp', 'expert')
Inputs may be any that keep to these rules, and one draw needn't show every extreme that they name: `route_ids`: of the 128 patches of one device, at most 6 are routed to one expert, and some device sends exactly 6 to one expert.
All inputs are finite; a program needn't handle non-finite values.
Results may differ from a plain program's by a relative error of at most 0.024.
Values may be sent and summed in bfloat16 or wider, within the bound.
A program may use at most 128 MiB of HBM per device.

v0:
```python
import jax
import jax.numpy as jnp
from jax import lax
from jax.sharding import PartitionSpec as P

HEADS = 16
RAD = 6


LN_EPS = 1e-05
ROOT_HALF = 0.7071067811865476
INV_ROOT_TAU = 0.3989422804014327
NEG_LARGE = -1e30


def padded(block, sides, width):
    for axis, dim in sides:
        count = lax.axis_size(axis)
        forward = [(i, i + 1) for i in range(count - 1)]
        backward = [(target, source) for source, target in forward]
        low = lax.ppermute(
            lax.slice_in_dim(block, block.shape[dim] - width, None, axis=dim), axis, forward
        )
        high = lax.ppermute(lax.slice_in_dim(block, 0, width, axis=dim), axis, backward)
        block = jnp.concatenate([low, block, high], axis=dim)
    return block


def gelu_value(values):
    return 0.5 * values * (1.0 + lax.erf(values * ROOT_HALF))


def gelu_slope(values):
    return (
        0.5 * (1.0 + lax.erf(values * ROOT_HALF))
        + values * jnp.exp(-0.5 * values * values) * INV_ROOT_TAU
    )


def layer_norm(stream, norm_gain):
    values = stream.astype(jnp.float32)
    center = values - jnp.mean(values, axis=-1, keepdims=True)
    inv_std = lax.rsqrt(jnp.mean(center * center, axis=-1, keepdims=True) + LN_EPS)
    normed = center * inv_std
    return (normed, inv_std, (normed * norm_gain).astype(jnp.bfloat16))


def norm_backward(grad_in, normed, inv_std, norm_gain):
    scaled = grad_in * norm_gain
    centered = scaled - jnp.mean(scaled, axis=-1, keepdims=True)
    return inv_std * (centered - normed * jnp.mean(scaled * normed, axis=-1, keepdims=True))


def expert_grads(rows_in, rows_grad, w_first, w_second):
    pre_act = jnp.dot(rows_in, w_first, preferred_element_type=jnp.float32)
    hidden = gelu_value(pre_act).astype(jnp.bfloat16)
    grad_hidden = lax.dot_general(
        rows_grad, w_second, (((1,), (1,)), ((), ())), preferred_element_type=jnp.float32
    )
    grad_pre = (grad_hidden * gelu_slope(pre_act)).astype(jnp.bfloat16)
    grad_second = lax.dot_general(
        hidden, rows_grad, (((0,), (0,)), ((), ())), preferred_element_type=jnp.float32
    )
    grad_first = lax.dot_general(
        rows_in, grad_pre, (((0,), (0,)), ((), ())), preferred_element_type=jnp.float32
    )
    back_terms = lax.dot_general(
        grad_pre, w_first, (((1,), (1,)), ((), ())), preferred_element_type=jnp.float32
    )
    return (grad_first.astype(jnp.bfloat16), grad_second.astype(jnp.bfloat16), back_terms)


def dispatch_table(routes, experts, capacity):
    tokens = routes.shape[0]
    onehot = (routes[:, None] == jnp.arange(experts, dtype=jnp.int32)[None, :]).astype(jnp.bfloat16)
    earlier = (jnp.arange(tokens)[:, None] > jnp.arange(tokens)[None, :]).astype(jnp.bfloat16)
    before = jnp.dot(earlier, onehot, preferred_element_type=jnp.float32)
    ranks = jnp.sum(before * onehot.astype(jnp.float32), axis=1).astype(jnp.int32)
    target = routes * capacity + ranks
    return (jnp.arange(experts * capacity, dtype=jnp.int32)[:, None] == target[None, :]).astype(
        jnp.bfloat16
    )


def fold_rims(grown, axis, inner):
    upper = lax.slice_in_dim(grown, 0, RAD, axis=axis)
    middle = lax.slice_in_dim(grown, 2 * RAD, 2 * RAD + inner, axis=axis)
    lower = lax.slice_in_dim(grown, inner + 3 * RAD, inner + 4 * RAD, axis=axis)
    widths_upper = [(0, 0)] * grown.ndim
    widths_lower = [(0, 0)] * grown.ndim
    widths_upper[axis] = (0, inner - RAD)
    widths_lower[axis] = (inner - RAD, 0)
    return middle + jnp.pad(upper, widths_upper) + jnp.pad(lower, widths_lower)


def window_mask(row_index, col_index, band, cols, first, count, ext_cols, rows_total, cols_total):
    own_rows = row_index * band + first + jnp.arange(count, dtype=jnp.int32)
    far_rows = row_index * band + first - RAD + jnp.arange(count + 2 * RAD, dtype=jnp.int32)
    own_cols = col_index * cols + jnp.arange(cols, dtype=jnp.int32)
    far_cols = col_index * cols - RAD + jnp.arange(ext_cols, dtype=jnp.int32)
    row_fine = (
        (jnp.abs(far_rows[None, :] - own_rows[:, None]) <= RAD)
        & (far_rows[None, :] >= 0)
        & (far_rows[None, :] < rows_total)
    )
    col_fine = (
        (jnp.abs(far_cols[None, :] - own_cols[:, None]) <= RAD)
        & (far_cols[None, :] >= 0)
        & (far_cols[None, :] < cols_total)
    )
    return (row_fine[:, None, :, None] & col_fine[None, :, None, :]).reshape(
        count * cols, (count + 2 * RAD) * ext_cols
    )


def body(
    query_act,
    key_act,
    value_act,
    stream,
    grad_out,
    norm_gain,
    route_ids,
    gate_prob,
    weight_in,
    weight_out,
):
    band, cols, width = stream.shape
    tokens = band * cols
    experts = lax.axis_size("dp")
    col_parts = lax.axis_size("expert")
    capacity = max(2, tokens * 3 // (2 * experts))
    head_size = width // HEADS
    ext_cols = cols + 2 * RAD
    block_rows = 4
    window_rows = block_rows + 2 * RAD
    block_count = band // block_rows
    joined = jnp.concatenate([key_act, value_act], axis=-1)
    grown = padded(joined, (("expert", 1), ("dp", 0)), RAD)
    flat_stream = stream.reshape(tokens, width)
    flat_grad = grad_out.reshape(tokens, width)
    normed, inv_std, expert_in = layer_norm(flat_stream, norm_gain)
    grad_z = (gate_prob.reshape(tokens, 1) * flat_grad.astype(jnp.float32)).astype(jnp.bfloat16)
    table = dispatch_table(route_ids.reshape(tokens), experts, capacity)
    slots_in = (
        jnp.dot(table, expert_in, preferred_element_type=jnp.float32)
        .astype(jnp.bfloat16)
        .reshape(experts, capacity, width)
    )
    slots_grad = (
        jnp.dot(table, grad_z, preferred_element_type=jnp.float32)
        .astype(jnp.bfloat16)
        .reshape(experts, capacity, width)
    )
    arrived_in, arrived_grad = (
        lax.all_to_all(slots_in, "dp", split_axis=0, concat_axis=0, tiled=True),
        lax.all_to_all(slots_grad, "dp", split_axis=0, concat_axis=0, tiled=True),
    )
    rows_in, rows_grad = (
        lax.all_gather(arrived_in, "expert", axis=0, tiled=True),
        lax.all_gather(arrived_grad, "expert", axis=0, tiled=True),
    )
    grad_first, grad_second, back_terms = expert_grads(
        rows_in.reshape(-1, width), rows_grad.reshape(-1, width), weight_in[0], weight_out[0]
    )
    own_terms = lax.psum_scatter(
        back_terms.reshape(col_parts, experts * capacity, width).astype(jnp.bfloat16),
        "expert",
        scatter_dimension=0,
        tiled=True,
    )
    returned = lax.all_to_all(
        own_terms.reshape(experts, capacity, width), "dp", split_axis=0, concat_axis=0, tiled=True
    )
    grad_u = lax.dot_general(
        table,
        returned.reshape(experts * capacity, width),
        (((0,), (0,)), ((), ())),
        preferred_element_type=jnp.float32,
    )
    grad_stream = (
        flat_grad.astype(jnp.float32) + norm_backward(grad_u, normed, inv_std, norm_gain)
    ).astype(jnp.bfloat16)
    grad_square = grad_stream.reshape(band, cols, width)
    row_index = lax.axis_index("dp")
    col_index = lax.axis_index("expert")
    rows_total = band * experts
    cols_total = cols * col_parts
    scale = head_size ** (-0.5)

    def forward_block(step, carry):
        query_acc, stats_acc, terms_acc = carry
        first = (step * block_rows).astype(jnp.int32)
        allowed = window_mask(
            row_index, col_index, band, cols, first, block_rows, ext_cols, rows_total, cols_total
        )
        queries = lax.dynamic_slice_in_dim(query_act, first, block_rows, 0).reshape(
            -1, HEADS, head_size
        )
        near = lax.dynamic_slice_in_dim(grown, first, window_rows, 0)
        keys_near = near[:, :, :width].reshape(-1, HEADS, head_size)
        values_near = near[:, :, width:].reshape(-1, HEADS, head_size)
        grad_heads = lax.dynamic_slice_in_dim(grad_square, first, block_rows, 0).reshape(
            -1, HEADS, head_size
        )
        scores = (
            jnp.einsum("qhd,khd->hqk", queries, keys_near, preferred_element_type=jnp.float32)
            * scale
        )
        masked = jnp.where(allowed[None], scores, NEG_LARGE)
        peak = jnp.max(masked, axis=-1, keepdims=True)
        log_total = peak + jnp.log(jnp.sum(jnp.exp(masked - peak), axis=-1, keepdims=True))
        probs = jnp.exp(masked - log_total)
        probs_low = probs.astype(jnp.bfloat16)
        attended = jnp.einsum(
            "hqk,khd->qhd", probs_low, values_near, preferred_element_type=jnp.float32
        )
        grad_probs = jnp.einsum(
            "qhd,khd->hqk", grad_heads, values_near, preferred_element_type=jnp.float32
        )
        delta = jnp.transpose(jnp.sum(grad_heads.astype(jnp.float32) * attended, axis=-1))
        grad_scores = (probs * (grad_probs - delta[:, :, None])).astype(jnp.bfloat16)
        grad_query = (
            jnp.einsum("hqk,khd->qhd", grad_scores, keys_near, preferred_element_type=jnp.float32)
            * scale
        )
        query_acc = lax.dynamic_update_slice_in_dim(
            query_acc, grad_query.reshape(block_rows, cols, width), first, 0
        )
        stats = jnp.transpose(jnp.concatenate([log_total[:, :, 0], delta], axis=0)).reshape(
            block_rows, cols, 2 * HEADS
        )
        stats_acc = lax.dynamic_update_slice_in_dim(stats_acc, stats, first, 0)
        key_terms = (
            jnp.einsum("hqk,qhd->khd", grad_scores, queries, preferred_element_type=jnp.float32)
            * scale
        )
        value_terms = jnp.einsum(
            "hqk,qhd->khd", probs_low, grad_heads, preferred_element_type=jnp.float32
        )
        both_terms = jnp.concatenate(
            [
                key_terms.reshape(window_rows, ext_cols, width),
                value_terms.reshape(window_rows, ext_cols, width),
            ],
            axis=-1,
        )
        previous = lax.dynamic_slice_in_dim(terms_acc, first, window_rows, 0)
        terms_acc = lax.dynamic_update_slice_in_dim(terms_acc, previous + both_terms, first, 0)
        return (query_acc, stats_acc, terms_acc)

    query_start = jnp.zeros((band, cols, width), jnp.float32)
    stats_start = jnp.zeros((band, cols, 2 * HEADS), jnp.float32)
    terms_start = jnp.zeros((band + 2 * RAD, ext_cols, 2 * width), jnp.float32)
    grad_query, stats_all, terms_all = lax.fori_loop(
        0, block_count, forward_block, (query_start, stats_start, terms_start)
    )
    received = padded(terms_all.astype(jnp.bfloat16), (("expert", 1), ("dp", 0)), RAD).astype(
        terms_all.dtype
    )
    summed = fold_rims(fold_rims(received, 0, band), 1, cols)
    grad_key = summed[:, :, :width]
    grad_value = summed[:, :, width:]
    return (
        grad_query.astype(jnp.bfloat16),
        grad_key.astype(jnp.bfloat16),
        grad_value.astype(jnp.bfloat16),
        grad_square,
        grad_first[None],
        grad_second[None],
    )


def solution(mesh):
    in_specs = (
        P("dp", "expert", None),
        P("dp", "expert", None),
        P("dp", "expert", None),
        P("dp", "expert", None),
        P("dp", "expert", None),
        P(),
        P("dp", "expert", None, None),
        P("dp", "expert", None),
        P("dp", None, "expert"),
        P("dp", "expert", None),
    )
    out_specs = (
        P("dp", "expert", None),
        P("dp", "expert", None),
        P("dp", "expert", None),
        P("dp", "expert", None),
        P("dp", None, "expert"),
        P("dp", "expert", None),
    )
    return jax.shard_map(body, mesh=mesh, in_specs=in_specs, out_specs=out_specs, check_vma=False)
```

profile of v0, /device:TPU:10, one launch (start us, length us, event | category | flops | bytes accessed | tf_op | source)
XLA Modules:
  0.0 619.5 jit_solution(17489740160623841284)
XLA Ops:
  12.5 33.6 %all_to_all.15 = bf16[32,6,1664]{2,1,0:T(8,128)(2,1)S(1)} all-to-all(bf16[32,6,1664]{2,1,0:T(8,128)(2,1)S(1)} %reshape.386), channel_id=1, replica_groups=mesh['expert'=8,'dp'=32] {'dp'}, dimensions={0} | all-to-all | bytes 1277952 | tf_op jit(solution)/shard_map/all_to_all | solution.py:157
  50.3 28.8 %all_to_all.16 = bf16[32,6,1664]{2,1,0:T(8,128)(2,1)S(1)} all-to-all(bf16[32,6,1664]{2,1,0:T(8,128)(2,1)S(1)} %reshape.388), channel_id=1, replica_groups=mesh['expert'=8,'dp'=32] {'dp'}, dimensions={0} | all-to-all | bytes 1277952 | tf_op jit(solution)/shard_map/all_to_all | solution.py:156
  83.3 8.2 %copy.72 = bf16[256,6,1664]{2,1,0:T(8,128)(2,1)} copy(bf16[256,6,1664]{2,0,1:T(8,128)(2,1)} %all-gather.3.cloned.1.call-done) | data formatting | bytes 10223616 | tf_op jit(solution)/shard_map/all_gather | solution.py:161
  91.4 9.4 %reshape.387 = bf16[1536,1664]{1,0:T(8,128)(2,1)} reshape(bf16[256,6,1664]{2,1,0:T(8,128)(2,1)} %copy.72) | data formatting | bytes 10223616 | tf_op jit(solution)/shard_map/reshape | solution.py:164
  100.9 23.4 %all-gather.5.cloned.1.call-done = bf16[256,6,1664]{2,0,1:T(8,128)(2,1)} async-done(((bf16[32,6,1664]{2,0,1:T(8,128)(2,1)}), bf16[256,6,1664]{2,0,1:T(8,128)(2,1)}) %all-gather.5.cloned.1.call-update) | async-done | bytes 5111824 | tf_op jit(solution)/shard_map/all_gather | solution.py:160
  124.3 8.2 %copy.74 = bf16[256,6,1664]{2,1,0:T(8,128)(2,1)} copy(bf16[256,6,1664]{2,0,1:T(8,128)(2,1)} %all-gather.5.cloned.1.call-done) | data formatting | bytes 10223616 | tf_op jit(solution)/shard_map/all_gather | solution.py:160
  132.4 9.4 %reshape.389 = bf16[1536,1664]{1,0:T(8,128)(2,1)} reshape(bf16[256,6,1664]{2,1,0:T(8,128)(2,1)} %copy.74) | data formatting | bytes 10223616 | tf_op jit(solution)/shard_map/reshape | solution.py:164
  141.9 5.0 fusion.30
  146.9 7.5 %fusion.23 = bf16[1536,512]{1,0:T(8,128)(2,1)S(1)} fusion(f32[1536,512]{1,0:T(8,128)S(1)} %fusion.30, bf16[1536,1664]{1,0:T(8,128)(2,1)} %reshape.387, bf16[1,512,1664]{2,1,0:T(8,128)(2,1)S(1)} %copy-done.13), kind=kOutput, calls=%fused_computation.56 | convolution fusion | flops 2625110016 | bytes 11534336 | tf_op jit(solution)/shard_map/dot_general | solution.py:57
  167.2 6.2 collective-permute-done
  178.7 5.2 collective-permute-start.3
  185.0 15.2 %collective-permute-start.2 = (bf16[6,20,3328]{2,1,0:T(8,128)(2,1)}, bf16[6,20,3328]{2,1,0:T(8,128)(2,1)}, u32[]{:S(2)}, u32[]{:S(2)}) collective-permute-start(bf16[6,20,3328]{2,1,0:T(8,128)(2,1)} %copy.67), channel_id=1, source_target_pairs={{0,1},{1,2},{2,3},{3,4},{4,5},{5,6},{6,7},{7,8},{8,9},{9,10},{10,1... | collective-permute-start | bytes 2396168 | tf_op jit(solution)/shard_map/ppermute | solution.py:21
  203.9 10.0 %all-to-all-start.2 = ((bf16[32,6,1664]{2,1,0:T(8,128)(2,1)}), bf16[32,6,1664]{2,1,0:T(8,128)(2,1)S(1)}, u32[]{:S(2)}, u32[]{:S(2)}) async-start(bf16[32,6,1664]{2,1,0:T(8,128)(2,1)} %reshape.390), calls=%async_computation.3 | async-start | bytes 1703936 | tf_op jit(solution)/shard_map/all_to_all | solution.py:172
  219.9 16.6 %all-to-all-done.2 = bf16[32,6,1664]{2,1,0:T(8,128)(2,1)S(1)} async-done(((bf16[32,6,1664]{2,1,0:T(8,128)(2,1)}), bf16[32,6,1664]{2,1,0:T(8,128)(2,1)S(1)}, u32[]{:S(2)}, u32[]{:S(2)}) %all-to-all-start.2) | async-done | bytes 639008 | tf_op jit(solution)/shard_map/all_to_all | solution.py:172
  244.6 278.5 %while.18 = (s32[]{:T(128)}, bf16[16,8,1664]{2,1,0:T(8,128)(2,1)}, f32[28,20,3328]{2,0,1:T(8,128)}, bf16[28,20,3328]{2,0,1:T(8,128)(2,1)}, s32[]{:T(128)}, /*ind...) while((s32[]{:T(128)}, bf16[16,8,1664]{2,1,0:T(8,128)(2,1)}, ...), condition=%wide.region_10.11_spmd, body=%wide.region_6.10_spmd.sunk | while | flops 209541376 | bytes 108690776 | solution.py:255
  298.7 15.7 %dynamic_update_slice.26 = f32[28,20,3328]{2,0,1:T(8,128)} dynamic-update-slice(f32[28,20,3328]{2,0,1:T(8,128)} %get-tuple-element.410, f32[16,20,3328]{2,0,1:T(8,128)} %copy.137, s32[]{:T(128)S(6)} %select_n.41, s32[]{:T(128)} %constant.168.clone.1..sunk, s32[]{:T(128)} %constant.168.clone.1..sunk) | dynamic-update-slice | bytes 8519684 | tf_op jit(solution)/shard_map/while/body/eval_jaxpr/dynamic_update_slice | solution.py:249
  368.4 15.8 %dynamic_update_slice.26 = f32[28,20,3328]{2,0,1:T(8,128)} dynamic-update-slice(f32[28,20,3328]{2,0,1:T(8,128)} %get-tuple-element.410, f32[16,20,3328]{2,0,1:T(8,128)} %copy.137, s32[]{:T(128)S(6)} %select_n.41, s32[]{:T(128)} %constant.168.clone.1..sunk, s32[]{:T(128)} %constant.168.clone.1..sunk) | dynamic-update-slice | bytes 8519684 | tf_op jit(solution)/shard_map/while/body/eval_jaxpr/dynamic_update_slice | solution.py:249
  438.3 15.3 %dynamic_update_slice.26 = f32[28,20,3328]{2,0,1:T(8,128)} dynamic-update-slice(f32[28,20,3328]{2,0,1:T(8,128)} %get-tuple-element.410, f32[16,20,3328]{2,0,1:T(8,128)} %copy.137, s32[]{:T(128)S(6)} %select_n.41, s32[]{:T(128)} %constant.168.clone.1..sunk, s32[]{:T(128)} %constant.168.clone.1..sunk) | dynamic-update-slice | bytes 8519684 | tf_op jit(solution)/shard_map/while/body/eval_jaxpr/dynamic_update_slice | solution.py:249
  507.7 15.4 %dynamic_update_slice.26 = f32[28,20,3328]{2,0,1:T(8,128)} dynamic-update-slice(f32[28,20,3328]{2,0,1:T(8,128)} %get-tuple-element.410, f32[16,20,3328]{2,0,1:T(8,128)} %copy.137, s32[]{:T(128)S(6)} %select_n.41, s32[]{:T(128)} %constant.168.clone.1..sunk, s32[]{:T(128)} %constant.168.clone.1..sunk) | dynamic-update-slice | bytes 8519684 | tf_op jit(solution)/shard_map/while/body/eval_jaxpr/dynamic_update_slice | solution.py:249
  533.1 13.0 %collective-permute-done.4 = bf16[28,6,3328]{2,0,1:T(8,128)(2,1)S(1)} collective-permute-done((bf16[28,6,3328]{2,0,1:T(8,128)(2,1)S(1)}, bf16[28,6,3328]{2,0,1:T(8,128)(2,1)S(1)}, u32[]{:S(2)}, u32[]{:S(2)}) %collective-permute-start.4) | collective-permute-done | bytes 1118240 | tf_op jit(solution)/shard_map/ppermute | solution.py:21
  549.2 5.4 collective-permute-start.7
  565.1 18.3 %collective-permute-done.7 = bf16[6,32,3328]{2,1,0:T(8,128)(2,1)S(1)} collective-permute-done((bf16[6,32,3328]{2,1,0:T(8,128)(2,1)S(1)}, bf16[6,32,3328]{2,1,0:T(8,128)(2,1)S(1)}, u32[]{:S(2)}, u32[]{:S(2)}) %collective-permute-start.7) | collective-permute-done | bytes 1277984 | tf_op jit(solution)/shard_map/ppermute | solution.py:24
  590.3 13.6 %maximum_convert_fusion = f32[40,32,3328]{2,0,1:T(8,128)} fusion(bf16[6,32,3328]{2,0,1:T(8,128)(2,1)S(1)} %copy.80, bf16[28,6,3328]{2,0,1:T(8,128)(2,1)S(1)} %collective-permute-done.5, bf16[28,20,3328]{2,0,1:T(8,128)(2,1)S(1)} %convert_element_type.130, bf16[28,6,3328]{2,0,1:T(8,128)(2,1)S(1)} %collective-permute-done.4, bf16[6,32,3328]{2,0,1:T(8,128)(2,1)S(1)} %copy.79), kind=kLoop, calls=%fused_computation.42 | loop fusion | flops 42598400 | bytes 25559040 | tf_op jit(solution)/shard_map/convert_element_type | solution.py:258
  603.8 6.7 %fusion.18 = f32[16,32,3328]{2,0,1:T(8,128)S(1)} fusion(f32[40,32,3328]{2,0,1:T(8,128)} %maximum_convert_fusion, f32[6,32,3328]{2,0,1:T(8,128)S(1)} %maximum_convert_fusion.1, pred[16]{0:T(512)(128)(4,1)S(1)} %copy-done.11), kind=kLoop, calls=%fused_computation.45 | loop fusion | flops 5111808 | bytes 23003152 | tf_op jit(solution)/shard_map/add | solution.py:93
  (281 shorter events, 298.7 us)
Async XLA Ops:
  7.2 134.7 %copy-start = (bf16[1,1664,512]{2,1,0:T(8,128)(2,1)S(1)}, bf16[1,1664,512]{2,1,0:T(8,128)(2,1)}, u32[]{:S(2)}) copy-start(bf16[1,1664,512]{2,1,0:T(8,128)(2,1)} %param.20) | copy-start | bytes 5111812
  7.2 76.1 %all-gather.3.cloned.1.call-start = ((), (), s32[]{:S(2)}) async-start(), calls=%async_computation.4 | async-start | bytes 5750784 | tf_op jit(solution)/shard_map/all_gather | solution.py:161
  8.8 38.2 %copy-start.5 = (bf16[16,8,1664]{2,1,0:T(8,128)(2,1)S(1)}, bf16[16,8,1664]{2,1,0:T(8,128)(2,1)}, u32[]{:S(2)}) copy-start(bf16[16,8,1664]{2,1,0:T(8,128)(2,1)} %param.15) | copy-start | bytes 1277956
  11.2 36.5 %copy-start.10 = (f32[1664]{0:T(1024)S(1)}, f32[1664]{0:T(1024)}, u32[]{:S(2)}) copy-start(f32[1664]{0:T(1024)} %param.17) | copy-start | bytes 19972
  47.0 77.2 %all-gather.5.cloned.1.call-start = ((), (), s32[]{:S(2)}) async-start(), calls=%async_computation.5 | async-start | bytes 5750784 | tf_op jit(solution)/shard_map/all_gather | solution.py:160
  80.0 121.8 %reduce-scatter.2.cloned.1.call-start = ((), (), s32[]{:S(2)}) async-start(), calls=%async_computation.6 | async-start | bytes 5750784 | tf_op jit(solution)/shard_map/reduce_scatter | solution.py:166
  146.9 7.5 %copy-start.16 = (f32[1536,512]{1,0:T(8,128)}, f32[1536,512]{1,0:T(8,128)S(1)}, u32[]{:S(2)}) copy-start(f32[1536,512]{1,0:T(8,128)S(1)} %fusion.30) | copy-start | bytes 9437188
  161.6 11.7 %collective-permute-start = (bf16[16,6,3328]{2,0,1:T(8,128)(2,1)S(1)}, bf16[16,6,3328]{2,0,1:T(8,128)(2,1)S(1)}, u32[]{:S(2)}, u32[]{:S(2)}) collective-permute-start(bf16[16,6,3328]{2,0,1:T(8,128)(2,1)S(1)} %get-tuple-element.312), channel_id=1, source_target_pairs={{0,32},{32,64},{64,96},{96,128},{128,160},{160,192},{192,224},{1,3... | collective-permute-start | bytes 1916936 | tf_op jit(solution)/shard_map/ppermute | solution.py:21
  163.8 13.3 %collective-permute-start.1 = (bf16[16,6,3328]{2,0,1:T(8,128)(2,1)S(1)}, bf16[16,6,3328]{2,0,1:T(8,128)(2,1)S(1)}, u32[]{:S(2)}, u32[]{:S(2)}) collective-permute-start(bf16[16,6,3328]{2,0,1:T(8,128)(2,1)S(1)} %get-tuple-element.313), channel_id=1, source_target_pairs={{32,0},{64,32},{96,64},{128,96},{160,128},{192,160},{224,192},{33,... | collective-permute-start | bytes 1916936 | tf_op jit(solution)/shard_map/ppermute | solution.py:24
  178.7 35.3 %collective-permute-start.3 = (bf16[6,20,3328]{2,1,0:T(8,128)(2,1)}, bf16[6,20,3328]{2,1,0:T(8,128)(2,1)}, u32[]{:S(2)}, u32[]{:S(2)}) collective-permute-start(bf16[6,20,3328]{2,1,0:T(8,128)(2,1)} %copy.68), channel_id=1, source_target_pairs={{1,0},{2,1},{3,2},{4,3},{5,4},{6,5},{7,6},{8,7},{9,8},{10,9},{11,1... | collective-permute-start | bytes 2396168 | tf_op jit(solution)/shard_map/ppermute | solution.py:24
  185.0 30.3 %collective-permute-start.2 = (bf16[6,20,3328]{2,1,0:T(8,128)(2,1)}, bf16[6,20,3328]{2,1,0:T(8,128)(2,1)}, u32[]{:S(2)}, u32[]{:S(2)}) collective-permute-start(bf16[6,20,3328]{2,1,0:T(8,128)(2,1)} %copy.67), channel_id=1, source_target_pairs={{0,1},{1,2},{2,3},{3,4},{4,5},{5,6},{6,7},{7,8},{8,9},{9,10},{10,1... | collective-permute-start | bytes 2396168 | tf_op jit(solution)/shard_map/ppermute | solution.py:21
  203.9 32.6 %all-to-all-start.2 = ((bf16[32,6,1664]{2,1,0:T(8,128)(2,1)}), bf16[32,6,1664]{2,1,0:T(8,128)(2,1)S(1)}, u32[]{:S(2)}, u32[]{:S(2)}) async-start(bf16[32,6,1664]{2,1,0:T(8,128)(2,1)} %reshape.390), calls=%async_computation.3 | async-start | bytes 1703936 | tf_op jit(solution)/shard_map/all_to_all | solution.py:172
  219.9 19.2 %copy-start.7 = (bf16[16,8,1664]{2,1,0:T(8,128)(2,1)S(1)}, bf16[16,8,1664]{2,1,0:T(8,128)(2,1)}, u32[]{:S(2)}) copy-start(bf16[16,8,1664]{2,1,0:T(8,128)(2,1)} %param.16) | copy-start | bytes 1277956
  523.1 33.6 %slice-start.2 = ((s8[5111808]{0:T(1024)(128)(4,1)}), s8[4194304]{0:T(1024)(128)(4,1)S(1)}, s32[]{:S(2)}) async-start(s8[5111808]{0:T(1024)(128)(4,1)} %bitcast.103), calls=%async_computation.9 | async-start | bytes 8388608
  527.3 29.4 %slice-start.3 = ((s8[5111808]{0:T(1024)(128)(4,1)}), s8[917504]{0:T(1024)(128)(4,1)S(1)}, s32[]{:S(2)}) async-start(s8[5111808]{0:T(1024)(128)(4,1)} %bitcast.103), calls=%async_computation.10 | async-start | bytes 1835008
  527.4 18.7 %collective-permute-start.4 = (bf16[28,6,3328]{2,0,1:T(8,128)(2,1)S(1)}, bf16[28,6,3328]{2,0,1:T(8,128)(2,1)S(1)}, u32[]{:S(2)}, u32[]{:S(2)}) collective-permute-start(bf16[28,6,3328]{2,0,1:T(8,128)(2,1)S(1)} %get-tuple-element.306), channel_id=1, source_target_pairs={{0,32},{32,64},{64,96},{96,128},{128,160},{160,192},{192,224},{1,3... | collective-permute-start | bytes 3354632 | tf_op jit(solution)/shard_map/ppermute | solution.py:21
  529.5 18.4 %collective-permute-start.5 = (bf16[28,6,3328]{2,0,1:T(8,128)(2,1)S(1)}, bf16[28,6,3328]{2,0,1:T(8,128)(2,1)S(1)}, u32[]{:S(2)}, u32[]{:S(2)}) collective-permute-start(bf16[28,6,3328]{2,0,1:T(8,128)(2,1)S(1)} %get-tuple-element.307), channel_id=1, source_target_pairs={{32,0},{64,32},{96,64},{128,96},{160,128},{192,160},{224,192},{33,... | collective-permute-start | bytes 3354632 | tf_op jit(solution)/shard_map/ppermute | solution.py:24
  548.7 8.0 %copy-start.15 = (bf16[1536,512]{1,0:T(8,128)(2,1)S(1)}, bf16[1536,512]{1,0:T(8,128)(2,1)}, u32[]{:S(2)}) copy-start(bf16[1536,512]{1,0:T(8,128)(2,1)} %copy-done.14) | copy-start | bytes 4718596
  548.9 11.9 %slice-start = ((s8[5111808]{0:T(1024)(128)(4,1)}), s8[4194304]{0:T(1024)(128)(4,1)S(1)}, s32[]{:S(2)}) async-start(s8[5111808]{0:T(1024)(128)(4,1)} %bitcast.101), calls=%async_computation.7 | async-start | bytes 8388608
  549.1 11.7 %slice-start.1 = ((s8[5111808]{0:T(1024)(128)(4,1)}), s8[917504]{0:T(1024)(128)(4,1)S(1)}, s32[]{:S(2)}) async-start(s8[5111808]{0:T(1024)(128)(4,1)} %bitcast.101), calls=%async_computation.8 | async-start | bytes 1835008
  549.2 11.7 %copy-start.17 = (f32[1536,512]{1,0:T(8,128)S(1)}, f32[1536,512]{1,0:T(8,128)}, u32[]{:S(2)}) copy-start(f32[1536,512]{1,0:T(8,128)} %copy-done.16) | copy-start | bytes 9437188
  549.2 34.2 %collective-permute-start.7 = (bf16[6,32,3328]{2,1,0:T(8,128)(2,1)S(1)}, bf16[6,32,3328]{2,1,0:T(8,128)(2,1)S(1)}, u32[]{:S(2)}, u32[]{:S(2)}) collective-permute-start(bf16[6,32,3328]{2,1,0:T(8,128)(2,1)S(1)} %copy.78), channel_id=1, source_target_pairs={{1,0},{2,1},{3,2},{4,3},{5,4},{6,5},{7,6},{8,7},{9,8},{10,9},{11,1... | collective-permute-start | bytes 3833864 | tf_op jit(solution)/shard_map/ppermute | solution.py:24
  554.6 34.2 %collective-permute-start.6 = (bf16[6,32,3328]{2,1,0:T(8,128)(2,1)S(1)}, bf16[6,32,3328]{2,1,0:T(8,128)(2,1)S(1)}, u32[]{:S(2)}, u32[]{:S(2)}) collective-permute-start(bf16[6,32,3328]{2,1,0:T(8,128)(2,1)S(1)} %copy.77), channel_id=1, source_target_pairs={{0,1},{1,2},{2,3},{3,4},{4,5},{5,6},{6,7},{7,8},{8,9},{9,10},{10,1... | collective-permute-start | bytes 3833864 | tf_op jit(solution)/shard_map/ppermute | solution.py:21
  590.3 13.6 %copy-start.11 = (pred[16]{0:T(512)(128)(4,1)S(1)}, pred[16]{0:T(512)(128)(4,1)}, u32[]{:S(2)}) copy-start(pred[16]{0:T(512)(128)(4,1)} %constant.184.clone.1) | copy-start | bytes 52
  (19 other events, 58.0 us)
Sparse Core Ops, SparseCore 0:
  47.1 36.0 all-gather.2
  85.7 38.5 all-gather.4
  160.5 41.2 reduce-scatter.1
where the time goes:
time: 626 us; the launch traced here: 619 us
  local copies, waits for them, and re-layouts  289 us (46%)
  waiting for transfers between devices  92 us (15%)
  matrix products  67.2 us (11%)
  blocking collectives  62.5 us (10%)
  starting transfers between devices  49.6 us (8%)
  other arithmetic  44.1 us (7%)
  between operations  14.4 us (2%)
    dynamic_update_slice x8, local copies, waits for them, and re-layouts, forward_block(): lax.dynamic_update_slice_in_dim(terms_acc, previous + both_terms, first, 0)  75.8 us
    all_to_all x1, blocking collectives, body(): lax.all_to_all(slots_grad, 'dp', split_axis=0, concat_axis=0, tiled=True)  33.6 us
    reshape x8, local copies, waits for them, and re-layouts, forward_block(): values_near = near[:, :, width:].reshape(-1, HEADS, head_size)  29.3 us
    all_to_all x1, blocking collectives, body(): lax.all_to_all(slots_in, 'dp', split_axis=0, concat_axis=0, tiled=True)  28.8 us
    ppermute x4, waiting for transfers between devices, padded(): lax.ppermute(lax.slice_in_dim(block, 0, width, axis=dim), axis, backward)  23.8 us
    ppermute x4, waiting for transfers between devices, padded(): lax.ppermute(lax.slice_in_dim(block, block.shape[dim] - width, None, axis...  23.8 us
    all_gather x1, waiting for transfers between devices, body(): lax.all_gather(arrived_in, 'expert', axis=0, tiled=True)  23.4 us
    ppermute x4, starting transfers between devices, padded(): lax.ppermute(lax.slice_in_dim(block, block.shape[dim] - width, None, axis...  21.5 us
  transfers between devices with their start and end apart: 12, of which 10 were waited for; matrix products, arithmetic and copies ran while one was open for 7% of the time, Pallas kernels for 0%

commit v1 on v0

v1 whole, which is shorter than its diff:
```python
import functools

import jax
import jax.numpy as jnp
from jax import lax
from jax.experimental import pallas as pl
from jax.experimental.pallas import tpu as pltpu
from jax.sharding import PartitionSpec as P

HEADS = 16
RAD = 6
VMEM_LIMIT = 48 * 1024 * 1024


LN_EPS = 1e-05
ROOT_HALF = 0.7071067811865476
INV_ROOT_TAU = 0.3989422804014327
NEG_LARGE = -1e30


def gelu_value(values):
    return 0.5 * values * (1.0 + lax.erf(values * ROOT_HALF))


def gelu_slope(values):
    return (
        0.5 * (1.0 + lax.erf(values * ROOT_HALF))
        + values * jnp.exp(-0.5 * values * values) * INV_ROOT_TAU
    )


def layer_norm(stream, norm_gain):
    values = stream.astype(jnp.float32)
    center = values - jnp.mean(values, axis=-1, keepdims=True)
    inv_std = lax.rsqrt(jnp.mean(center * center, axis=-1, keepdims=True) + LN_EPS)
    normed = center * inv_std
    return (normed, inv_std, (normed * norm_gain).astype(jnp.bfloat16))


def norm_backward(grad_in, normed, inv_std, norm_gain):
    scaled = grad_in * norm_gain
    centered = scaled - jnp.mean(scaled, axis=-1, keepdims=True)
    return inv_std * (centered - normed * jnp.mean(scaled * normed, axis=-1, keepdims=True))


def expert_grads(rows_in, rows_grad, w_first, w_second):
    pre_act = jnp.dot(rows_in, w_first, preferred_element_type=jnp.float32)
    hidden = gelu_value(pre_act).astype(jnp.bfloat16)
    grad_hidden = lax.dot_general(
        rows_grad, w_second, (((1,), (1,)), ((), ())), preferred_element_type=jnp.float32
    )
    grad_pre = (grad_hidden * gelu_slope(pre_act)).astype(jnp.bfloat16)
    grad_second = lax.dot_general(
        hidden, rows_grad, (((0,), (0,)), ((), ())), preferred_element_type=jnp.float32
    )
    grad_first = lax.dot_general(
        rows_in, grad_pre, (((0,), (0,)), ((), ())), preferred_element_type=jnp.float32
    )
    back_terms = lax.dot_general(
        grad_pre, w_first, (((1,), (1,)), ((), ())), preferred_element_type=jnp.float32
    )
    return (grad_first.astype(jnp.bfloat16), grad_second.astype(jnp.bfloat16), back_terms)


def dispatch_table(routes, experts, capacity):
    tokens = routes.shape[0]
    onehot = (routes[:, None] == jnp.arange(experts, dtype=jnp.int32)[None, :]).astype(jnp.bfloat16)
    earlier = (jnp.arange(tokens)[:, None] > jnp.arange(tokens)[None, :]).astype(jnp.bfloat16)
    before = jnp.dot(earlier, onehot, preferred_element_type=jnp.float32)
    ranks = jnp.sum(before * onehot.astype(jnp.float32), axis=1).astype(jnp.int32)
    target = routes * capacity + ranks
    return (jnp.arange(experts * capacity, dtype=jnp.int32)[:, None] == target[None, :]).astype(
        jnp.bfloat16
    )


def head_lanes(head, size, width):
    start = head * size
    low = start // 128 * 128
    high = min((start + size + 127) // 128 * 128, width)
    return start, low, high


def lane_mask(head, size, low, high):
    lanes = lax.broadcasted_iota(jnp.int32, (1, high - low), 1) + low
    return (lanes >= head * size) & (lanes < (head + 1) * size)


def nt_dot(left, right):
    return lax.dot_general(left, right, (((1,), (1,)), ((), ())), preferred_element_type=jnp.float32)


def nn_dot(left, right):
    return jnp.dot(left, right, preferred_element_type=jnp.float32)


def window_bias(band, cols, rows_total, cols_total):
    row_index = lax.axis_index("dp")
    col_index = lax.axis_index("expert")
    side = (band + 2 * RAD) * cols
    shape = (band * cols, 3 * side)
    shift = cols.bit_length() - 1
    own = lax.broadcasted_iota(jnp.int32, shape, 0)
    far = lax.broadcasted_iota(jnp.int32, shape, 1)
    part = (far >= side).astype(jnp.int32) + (far >= 2 * side).astype(jnp.int32)
    within = far - side * part
    far_row = (within >> shift) - RAD
    far_col = (within & (cols - 1)) + cols * (part - 1)
    own_row = own >> shift
    own_col = own & (cols - 1)
    abs_row = far_row + row_index * band
    abs_col = far_col + col_index * cols
    fine = (
        (jnp.abs(far_row - own_row) <= RAD)
        & (jnp.abs(far_col - own_col) <= RAD)
        & (abs_row >= 0)
        & (abs_row < rows_total)
        & (abs_col >= 0)
        & (abs_col < cols_total)
    )
    return jnp.where(fine, 0.0, NEG_LARGE)


def tall(refs, low, high):
    return jnp.concatenate([ref[:, low:high] for ref in refs], axis=0)


def forward_kernel(sizes, query_ref, left_ref, mid_ref, right_ref, att_ref, stats_ref, bias_ref):
    band, cols, rows_total, cols_total = sizes
    width = query_ref.shape[1]
    size = width // HEADS
    scale = size ** (-0.5)
    refs = (left_ref, mid_ref, right_ref)
    bias_ref[...] = window_bias(band, cols, rows_total, cols_total)
    att_ref[...] = jnp.zeros_like(att_ref)
    lanes = lax.broadcasted_iota(jnp.int32, stats_ref.shape, 1)
    stats = jnp.zeros(stats_ref.shape, jnp.float32)
    for head in range(HEADS):
        start, low, high = head_lanes(head, size, width)
        mask = lane_mask(head, size, low, high)
        queries = query_ref[:, low:high] * mask.astype(jnp.bfloat16)
        scores = nt_dot(queries, tall(refs, low, high)) * scale + bias_ref[...]
        peak = jnp.max(scores, axis=-1, keepdims=True)
        log_total = peak + jnp.log(jnp.sum(jnp.exp(scores - peak), axis=-1, keepdims=True))
        probs_low = jnp.exp(scores - log_total).astype(jnp.bfloat16)
        attended = nn_dot(probs_low, tall(refs, width + low, width + high))
        att_ref[:, low:high] += jnp.where(mask, attended, 0.0)
        stats = jnp.where(lanes == head, log_total, stats)
    stats_ref[...] = stats


def split_three(values):
    first = values.astype(jnp.bfloat16)
    rest = values - first.astype(jnp.float32)
    second = rest.astype(jnp.bfloat16)
    third = (rest - second.astype(jnp.float32)).astype(jnp.bfloat16)
    return first, second, third


def stream_kernel(stream_ref, grad_ref, gain_ref, back_ref, att_ref, stats_ref, plain_ref, packed_ref):
    width = stream_ref.shape[1]
    size = width // HEADS
    gain = gain_ref[...]
    normed, inv_std, _ = layer_norm(stream_ref[...], gain)
    grad_stream = (
        grad_ref[...].astype(jnp.float32) + norm_backward(back_ref[...], normed, inv_std, gain)
    ).astype(jnp.bfloat16)
    plain_ref[...] = grad_stream
    packed_ref[:, :width] = grad_stream
    products = grad_stream.astype(jnp.float32) * att_ref[...]
    feature = lax.broadcasted_iota(jnp.int32, (width, 128), 0)
    first = lax.broadcasted_iota(jnp.int32, (width, 128), 1) * size
    owner = jnp.where((feature >= first) & (feature < first + size), 1.0, 0.0).astype(jnp.bfloat16)
    delta = sum(nn_dot(piece, owner) for piece in split_three(products))
    source = lax.broadcasted_iota(jnp.int32, (128, 128), 0)
    target = lax.broadcasted_iota(jnp.int32, (128, 128), 1)
    total = jnp.zeros(delta.shape, jnp.float32)
    pieces = split_three(stats_ref[...]) + split_three(delta)
    for place, piece in enumerate(pieces):
        move = (target == source + place * HEADS) & (source < HEADS)
        total = total + nn_dot(piece, jnp.where(move, 1.0, 0.0).astype(jnp.bfloat16))
    packed_ref[:, width:] = total.astype(jnp.bfloat16)


def backward_kernel(
    sizes,
    left_ref,
    mid_ref,
    right_ref,
    gleft_ref,
    gmid_ref,
    gright_ref,
    gq_ref,
    gk_ref,
    gv_ref,
    bias_ref,
    acc_q,
    acc_k,
    acc_v,
):
    band, cols, rows_total, cols_total = sizes
    width = gq_ref.shape[1]
    size = width // HEADS
    scale = size ** (-0.5)
    tokens = band * cols
    own = slice(RAD * cols, RAD * cols + tokens)
    refs = (left_ref, mid_ref, right_ref)
    grefs = (gleft_ref, gmid_ref, gright_ref)
    bias_ref[...] = window_bias(band, cols, rows_total, cols_total)
    for acc in (acc_q, acc_k, acc_v):
        acc[...] = jnp.zeros_like(acc)
    row = lax.broadcasted_iota(jnp.int32, (2 * HEADS, 128), 0)
    lane = lax.broadcasted_iota(jnp.int32, (2 * HEADS, 128), 1)
    base = jnp.where(row < HEADS, row, row + 2 * HEADS)
    pick = jnp.where(
        (lane == base) | (lane == base + HEADS) | (lane == base + 2 * HEADS), 1.0, 0.0
    ).astype(jnp.bfloat16)
    stats_far = nt_dot(pick, tall(grefs, width, width + 128))
    stats_own = nt_dot(gmid_ref[own, width : width + 128], pick)
    for head in range(HEADS):
        start, low, high = head_lanes(head, size, width)
        mask = lane_mask(head, size, low, high)
        mask_low = mask.astype(jnp.bfloat16)
        keys = tall(refs, low, high)
        values = tall(refs, width + low, width + high)
        queries = tall(refs, 2 * width + low, 2 * width + high)
        grads = tall(grefs, low, high)
        bias = bias_ref[...]
        own_key = mid_ref[own, low:high] * mask_low
        own_value = mid_ref[own, width + low : width + high] * mask_low
        own_query = mid_ref[own, 2 * width + low : 2 * width + high] * mask_low
        own_grad = gmid_ref[own, low:high] * mask_low

        probs = jnp.exp(
            nt_dot(own_query, keys) * scale + bias - stats_own[:, head : head + 1]
        )
        grad_probs = nt_dot(own_grad, values)
        grad_scores = (
            probs * (grad_probs - stats_own[:, HEADS + head : HEADS + head + 1])
        ).astype(jnp.bfloat16)
        acc_q[:, low:high] += jnp.where(mask, nn_dot(grad_scores, keys), 0.0)

        probs = jnp.exp(
            nt_dot(own_key, queries) * scale + bias - stats_far[head : head + 1, :]
        )
        acc_v[:, low:high] += jnp.where(mask, nn_dot(probs.astype(jnp.bfloat16), grads), 0.0)
        grad_probs = nt_dot(own_value, grads)
        grad_scores = (
            probs * (grad_probs - stats_far[HEADS + head : HEADS + head + 1, :])
        ).astype(jnp.bfloat16)
        acc_k[:, low:high] += jnp.where(mask, nn_dot(grad_scores, queries), 0.0)
    gq_ref[...] = (acc_q[...] * scale).astype(jnp.bfloat16)
    gk_ref[...] = (acc_k[...] * scale).astype(jnp.bfloat16)
    gv_ref[...] = acc_v[...].astype(jnp.bfloat16)


def vmem():
    return pl.BlockSpec(memory_space=pltpu.VMEM)


def wide_halo(block, rim):
    def pairs(axis):
        count = lax.axis_size(axis)
        forward = [(i, i + 1) for i in range(count - 1)]
        return forward, [(b, a) for a, b in forward]

    forward, backward = pairs("dp")
    upper = lax.ppermute(block[block.shape[0] - rim :], "dp", forward)
    lower = lax.ppermute(block[:rim], "dp", backward)
    mid = jnp.concatenate([upper, block, lower], axis=0)
    forward, backward = pairs("expert")
    left = lax.ppermute(mid, "expert", forward)
    right = lax.ppermute(mid, "expert", backward)
    return left, mid, right

def body(
    query_act,
    key_act,
    value_act,
    stream,
    grad_out,
    norm_gain,
    route_ids,
    gate_prob,
    weight_in,
    weight_out,
):
    band, cols, width = stream.shape
    tokens = band * cols
    experts = lax.axis_size("dp")
    col_parts = lax.axis_size("expert")
    capacity = max(2, tokens * 3 // (2 * experts))
    sizes = (band, cols, band * experts, cols * col_parts)
    side = (band + 2 * RAD) * cols
    flat_query = query_act.reshape(tokens, width)
    joined = jnp.concatenate(
        [key_act.reshape(tokens, width), value_act.reshape(tokens, width), flat_query], axis=-1
    )
    near = wide_halo(joined, RAD * cols)
    attended, log_total = pl.pallas_call(
        functools.partial(forward_kernel, sizes),
        out_shape=(
            jax.ShapeDtypeStruct((tokens, width), jnp.float32),
            jax.ShapeDtypeStruct((tokens, 128), jnp.float32),
        ),
        in_specs=[vmem()] * 4,
        out_specs=(vmem(), vmem()),
        scratch_shapes=[pltpu.VMEM((tokens, 3 * side), jnp.float32)],
        compiler_params=pltpu.CompilerParams(vmem_limit_bytes=VMEM_LIMIT),
        name="attend",
    )(flat_query, *near)
    flat_stream = stream.reshape(tokens, width)
    flat_grad = grad_out.reshape(tokens, width)
    normed, inv_std, expert_in = layer_norm(flat_stream, norm_gain)
    grad_z = (gate_prob.reshape(tokens, 1) * flat_grad.astype(jnp.float32)).astype(jnp.bfloat16)
    table = dispatch_table(route_ids.reshape(tokens), experts, capacity)
    slots_in = (
        jnp.dot(table, expert_in, preferred_element_type=jnp.float32)
        .astype(jnp.bfloat16)
        .reshape(experts, capacity, width)
    )
    slots_grad = (
        jnp.dot(table, grad_z, preferred_element_type=jnp.float32)
        .astype(jnp.bfloat16)
        .reshape(experts, capacity, width)
    )
    arrived_in, arrived_grad = (
        lax.all_to_all(slots_in, "dp", split_axis=0, concat_axis=0, tiled=True),
        lax.all_to_all(slots_grad, "dp", split_axis=0, concat_axis=0, tiled=True),
    )
    rows_in, rows_grad = (
        lax.all_gather(arrived_in, "expert", axis=0, tiled=True),
        lax.all_gather(arrived_grad, "expert", axis=0, tiled=True),
    )
    grad_first, grad_second, back_terms = expert_grads(
        rows_in.reshape(-1, width), rows_grad.reshape(-1, width), weight_in[0], weight_out[0]
    )
    own_terms = lax.psum_scatter(
        back_terms.reshape(col_parts, experts * capacity, width).astype(jnp.bfloat16),
        "expert",
        scatter_dimension=0,
        tiled=True,
    )
    returned = lax.all_to_all(
        own_terms.reshape(experts, capacity, width), "dp", split_axis=0, concat_axis=0, tiled=True
    )
    grad_u = lax.dot_general(
        table,
        returned.reshape(experts * capacity, width),
        (((0,), (0,)), ((), ())),
        preferred_element_type=jnp.float32,
    )
    plain, packed = pl.pallas_call(
        stream_kernel,
        out_shape=(
            jax.ShapeDtypeStruct((tokens, width), jnp.bfloat16),
            jax.ShapeDtypeStruct((tokens, width + 128), jnp.bfloat16),
        ),
        in_specs=[vmem()] * 6,
        out_specs=(vmem(), vmem()),
        compiler_params=pltpu.CompilerParams(vmem_limit_bytes=VMEM_LIMIT),
        name="stream_grad",
    )(flat_stream, flat_grad, norm_gain.reshape(1, width), grad_u, attended, log_total)
    far = wide_halo(packed, RAD * cols)
    grad_query, grad_key, grad_value = pl.pallas_call(
        functools.partial(backward_kernel, sizes),
        out_shape=(jax.ShapeDtypeStruct((tokens, width), jnp.bfloat16),) * 3,
        in_specs=[vmem()] * 6,
        out_specs=(vmem(),) * 3,
        scratch_shapes=[pltpu.VMEM((tokens, 3 * side), jnp.float32)]
        + [pltpu.VMEM((tokens, width), jnp.float32)] * 3,
        compiler_params=pltpu.CompilerParams(vmem_limit_bytes=VMEM_LIMIT),
        name="attend_back",
    )(*near, *far)
    shape = (band, cols, width)
    return (
        grad_query.reshape(shape),
        grad_key.reshape(shape),
        grad_value.reshape(shape),
        plain.reshape(shape),
        grad_first[None],
        grad_second[None],
    )


def solution(mesh):
    in_specs = (
        P("dp", "expert", None),
        P("dp", "expert", None),
        P("dp", "expert", None),
        P("dp", "expert", None),
        P("dp", "expert", None),
        P(),
        P("dp", "expert", None, None),
        P("dp", "expert", None),
        P("dp", None, "expert"),
        P("dp", "expert", None),
    )
    out_specs = (
        P("dp", "expert", None),
        P("dp", "expert", None),
        P("dp", "expert", None),
        P("dp", "expert", None),
        P("dp", None, "expert"),
        P("dp", "expert", None),
    )
    return jax.shard_map(body, mesh=mesh, in_specs=in_specs, out_specs=out_specs, check_vma=False)
```

time: 626 us -> 309 us (0.49)
  the two profiles are of different devices: /device:TPU:10 before, /device:TPU:24 now
where the time goes in v1:
time: 309 us; the launch traced here: 305 us
  waiting for transfers between devices  74.1 us (24%)
  blocking collectives  64.7 us (21%)
  local copies, waits for them, and re-layouts  46.8 us (15%)
  starting transfers between devices  38.2 us (12%)
  matrix products  32.8 us (11%)
  Pallas kernels  26.8 us (9%)
  between operations  14.4 us (5%)
  other arithmetic  7.57 us (2%)
    all_to_all x1, blocking collectives, body(): lax.all_to_all(slots_grad, 'dp', split_axis=0, concat_axis=0, tiled=True)  35.9 us
    all_to_all x1, blocking collectives, body(): lax.all_to_all(slots_in, 'dp', split_axis=0, concat_axis=0, tiled=True)  28.8 us
    all_gather x1, waiting for transfers between devices, body(): lax.all_gather(arrived_in, 'expert', axis=0, tiled=True)  22.8 us
    pallas_call x1, Pallas kernels, body(): pl.pallas_call(functools.partial(backward_kernel, sizes), out_shape=(jax....  15.7 us
    reduce_scatter x1, waiting for transfers between devices, body(): lax.psum_scatter(back_terms.reshape(col_parts, experts * capacity, width)...  15.7 us
    all_to_all x1, starting transfers between devices, body(): lax.all_to_all(own_terms.reshape(experts, capacity, width), 'dp', split_a...  10.9 us
    ppermute x2, starting transfers between devices, wide_halo(): right = lax.ppermute(mid, 'expert', backward)  10.7 us
    ppermute x2, waiting for transfers between devices, wide_halo(): lower = lax.ppermute(block[:rim], 'dp', backward)  10.1 us
  transfers between devices with their start and end apart: 12, of which 10 were waited for; matrix products, arithmetic and copies ran while one was open for 13% of the time, Pallas kernels for 3%

profile of v1, /device:TPU:24, one launch (start us, length us, event | category | flops | bytes accessed | tf_op | source)
XLA Modules:
  0.0 305.3 jit_solution(16427415665934562164)
XLA Ops:
  12.5 35.9 %all_to_all.15 = bf16[32,6,1664]{2,1,0:T(8,128)(2,1)S(1)} all-to-all(bf16[32,6,1664]{2,1,0:T(8,128)(2,1)S(1)} %reshape.117), channel_id=1, replica_groups=mesh['expert'=8,'dp'=32] {'dp'}, dimensions={0} | all-to-all | bytes 1277952 | tf_op jit(solution)/shard_map/all_to_all | solution.py:329
  52.5 28.8 %all_to_all.16 = bf16[32,6,1664]{2,1,0:T(8,128)(2,1)S(1)} all-to-all(bf16[32,6,1664]{2,1,0:T(8,128)(2,1)S(1)} %reshape.119), channel_id=1, replica_groups=mesh['expert'=8,'dp'=32] {'dp'}, dimensions={0} | all-to-all | bytes 1277952 | tf_op jit(solution)/shard_map/all_to_all | solution.py:328
  82.8 8.2 %copy.17 = bf16[256,6,1664]{2,1,0:T(8,128)(2,1)} copy(bf16[256,6,1664]{2,0,1:T(8,128)(2,1)} %all-gather.3.cloned.1.call-done) | data formatting | bytes 10223616 | tf_op jit(solution)/shard_map/all_gather | solution.py:333
  91.0 9.5 %reshape.118 = bf16[1536,1664]{1,0:T(8,128)(2,1)} reshape(bf16[256,6,1664]{2,1,0:T(8,128)(2,1)} %copy.17) | data formatting | bytes 10223616 | tf_op jit(solution)/shard_map/reshape | solution.py:336
  100.4 22.8 %all-gather.5.cloned.1.call-done = bf16[256,6,1664]{2,0,1:T(8,128)(2,1)} async-done(((bf16[32,6,1664]{2,0,1:T(8,128)(2,1)}), bf16[256,6,1664]{2,0,1:T(8,128)(2,1)}) %all-gather.5.cloned.1.call-update) | async-done | bytes 5111824 | tf_op jit(solution)/shard_map/all_gather | solution.py:332
  123.2 8.2 %copy.19 = bf16[256,6,1664]{2,1,0:T(8,128)(2,1)} copy(bf16[256,6,1664]{2,0,1:T(8,128)(2,1)} %all-gather.5.cloned.1.call-done) | data formatting | bytes 10223616 | tf_op jit(solution)/shard_map/all_gather | solution.py:332
  131.4 9.4 %reshape.120 = bf16[1536,1664]{1,0:T(8,128)(2,1)} reshape(bf16[256,6,1664]{2,1,0:T(8,128)(2,1)} %copy.19) | data formatting | bytes 10223616 | tf_op jit(solution)/shard_map/reshape | solution.py:336
  140.8 5.0 %fusion.8 = f32[1536,512]{1,0:T(8,128)S(1)} fusion(bf16[1536,1664]{1,0:T(8,128)(2,1)} %reshape.120, bf16[1,1664,512]{2,1,0:T(8,128)(2,1)S(1)} %copy-done), kind=kOutput, calls=%fused_computation.18 | convolution fusion | flops 2617245696 | bytes 9961472 | tf_op jit(solution)/shard_map/dot_general | solution.py:47
  145.8 7.5 %fusion.4 = bf16[1536,512]{1,0:T(8,128)(2,1)S(1)} fusion(f32[1536,512]{1,0:T(8,128)S(1)} %fusion.8, bf16[1536,1664]{1,0:T(8,128)(2,1)} %reshape.118, bf16[1,512,1664]{2,1,0:T(8,128)(2,1)S(1)} %copy-done.11), kind=kOutput, calls=%fused_computation.9 | convolution fusion | flops 2625110016 | bytes 11534336 | tf_op jit(solution)/shard_map/dot_general | solution.py:49
  154.5 4.7 %convolution_convert_fusion = bf16[8,192,1664]{2,1,0:T(8,128)(2,1)} fusion(bf16[8,192,512]{2,1,0:T(8,128)(2,1)S(1)} %bitcast.58, bf16[1,1664,512]{2,1,0:T(8,128)(2,1)S(1)} %copy-done), kind=kOutput, calls=%fused_computation.1 | convolution fusion | flops 2619801600 | bytes 8388608 | tf_op jit(solution)/shard_map/dot_general | solution.py:59
  165.5 9.1 %collective-permute-done = bf16[48,4992]{1,0:T(8,128)(2,1)S(1)} collective-permute-done((bf16[48,4992]{1,0:T(8,128)(2,1)S(1)}, bf16[48,4992]{1,0:T(8,128)(2,1)S(1)}, u32[]{:S(2)}, u32[]{:S(2)}) %collective-permute-start) | collective-permute-done | bytes 479264 | tf_op jit(solution)/shard_map/ppermute | solution.py:268
  174.7 4.1 %collective-permute-done.1 = bf16[48,4992]{1,0:T(8,128)(2,1)S(1)} collective-permute-done((bf16[48,4992]{1,0:T(8,128)(2,1)S(1)}, bf16[48,4992]{1,0:T(8,128)(2,1)S(1)}, u32[]{:S(2)}, u32[]{:S(2)}) %collective-permute-start.1) | collective-permute-done | bytes 479264 | tf_op jit(solution)/shard_map/ppermute | solution.py:269
  178.8 6.4 %pad_maximum_fusion.mid_ref = bf16[224,4992]{1,0:T(8,128)(2,1)S(1)} fusion(bf16[48,4992]{1,0:T(8,128)(2,1)S(1)} %collective-permute-done.1, bf16[128,1664]{1,0:T(8,128)(2,1)S(1)} %bitcast.43, bf16[128,1664]{1,0:T(8,128)(2,1)S(1)} %bitcast.49, bf16[128,1664]{1,0:T(8,128)(2,1)} %bitcast.50, bf16[48,4992]{1,0:T(8,128)(2,1)S(1)} %collective-permute-done), kind=kLoop, calls=%fused_computation.16 | loop fusion | flops 11182080 | bytes 4472832 | tf_op jit(solution)/shard_map/concatenate | solution.py:270
  190.9 15.7 %reduce-scatter.2.cloned.1.call-done = bf16[1,192,1664]{2,1,0:T(8,128)(2,1)} async-done(((bf16[8,192,1664]{2,1,0:T(8,128)(2,1)}), bf16[1,192,1664]{2,1,0:T(8,128)(2,1)}) %reduce-scatter.2.cloned.1.call-update) | async-done | bytes 638992 | tf_op jit(solution)/shard_map/reduce_scatter | solution.py:338
  208.7 10.9 %all-to-all-start.2 = ((bf16[32,6,1664]{2,1,0:T(8,128)(2,1)}), bf16[32,6,1664]{2,1,0:T(8,128)(2,1)}, u32[]{:S(2)}, u32[]{:S(2)}) async-start(bf16[32,6,1664]{2,1,0:T(8,128)(2,1)} %reshape.121), calls=%async_computation.3 | async-start | bytes 1703936 | tf_op jit(solution)/shard_map/all_to_all | solution.py:344
  222.2 9.1 %attend.1 = (f32[128,1664]{1,0:T(8,128)S(1)}, f32[128,128]{1,0:T(8,128)S(1)}) custom-call(bf16[128,1664]{1,0:T(8,128)(2,1)S(1)} %bitcast.44, bf16[224,4992]{1,0:T(8,128)(2,1)} %collective-permute-done.2.left_ref, bf16[224,4992]{1,0:T(8,128)(2,1)S(1)} %pad_maximum_fusion.mid_ref, bf16[224,4992]{1,0:T(8,128)(2,1)} %collective-permute-done.3.right_ref), custom_call_target="tpu_custom_call" | custom-call | tf_op jit(solution)/shard_map/attend/pallas_call | solution.py:300
  232.3 6.7 %all-to-all-done.2 = bf16[32,6,1664]{2,1,0:T(8,128)(2,1)} async-done(((bf16[32,6,1664]{2,1,0:T(8,128)(2,1)}), bf16[32,6,1664]{2,1,0:T(8,128)(2,1)}, u32[]{:S(2)}, u32[]{:S(2)}) %all-to-all-start.2) | async-done | bytes 639008 | tf_op jit(solution)/shard_map/all_to_all | solution.py:344
  242.9 4.2 %collective-permute-start.4 = (bf16[48,1792]{1,0:T(8,128)(2,1)S(1)}, bf16[48,1792]{1,0:T(8,128)(2,1)S(1)}, u32[]{:S(2)}, u32[]{:S(2)}) collective-permute-start(bf16[48,1792]{1,0:T(8,128)(2,1)S(1)} %get-tuple-element.23), channel_id=1, source_target_pairs={{0,1},{1,2},{2,3},{3,4},{4,5},{5,6},{6,7},{7,8},{8,9},{9,10},{10,1... | collective-permute-start | bytes 516104 | tf_op jit(solution)/shard_map/ppermute | solution.py:268
  247.1 6.5 %fusion.5 = bf16[1,1664,512]{2,1,0:T(8,128)(2,1)} fusion(bf16[1536,1664]{1,0:T(8,128)(2,1)} %reshape.120, bf16[1536,512]{1,0:T(8,128)(2,1)S(1)} %copy-done.13), kind=kOutput, calls=%fused_computation.12 | convolution fusion | flops 2618097664 | bytes 8388608 | tf_op jit(solution)/shard_map/dot_general | solution.py:56
  254.9 5.9 %collective-permute-done.5 = bf16[48,1792]{1,0:T(8,128)(2,1)S(1)} collective-permute-done((bf16[48,1792]{1,0:T(8,128)(2,1)S(1)}, bf16[48,1792]{1,0:T(8,128)(2,1)S(1)}, u32[]{:S(2)}, u32[]{:S(2)}) %collective-permute-start.5) | collective-permute-done | bytes 172064 | tf_op jit(solution)/shard_map/ppermute | solution.py:269
  260.8 8.5 %collective-permute-start.7 = (bf16[224,1792]{1,0:T(8,128)(2,1)S(1)}, bf16[224,1792]{1,0:T(8,128)(2,1)S(1)}, u32[]{:S(2)}, u32[]{:S(2)}) collective-permute-start(bf16[224,1792]{1,0:T(8,128)(2,1)S(1)} %constant_dynamic-update-slice_fusion.gmid_ref), channel_id=1, source_target_pairs={{32,0},{64,32},{96,64},{128,96},{160,128},{192,160},{224,192},{33,... | collective-permute-start | bytes 2408456 | tf_op jit(solution)/shard_map/ppermute | solution.py:273
  271.5 4.2 %fusion.6 = bf16[1,512,1664]{2,1,0:T(8,128)(2,1)} fusion(bf16[1536,1664]{1,0:T(8,128)(2,1)S(1)} %bitcast.47, f32[1536,512]{1,0:T(8,128)S(1)} %copy-done.15), kind=kOutput, calls=%fused_computation.13 | convolution fusion | flops 2622029824 | bytes 9961472 | tf_op jit(solution)/shard_map/dot_general | solution.py:53
  279.0 3.8 %collective-permute-done.6.gleft_ref = bf16[224,1792]{1,0:T(8,128)(2,1)S(1)} collective-permute-done((bf16[224,1792]{1,0:T(8,128)(2,1)S(1)}, bf16[224,1792]{1,0:T(8,128)(2,1)S(1)}, u32[]{:S(2)}, u32[]{:S(2)}) %collective-permute-start.6) | collective-permute-done | bytes 802848 | tf_op jit(solution)/shard_map/ppermute | solution.py:272
  282.8 15.7 %attend_back.1 = (bf16[128,1664]{1,0:T(8,128)(2,1)}, bf16[128,1664]{1,0:T(8,128)(2,1)}, bf16[128,1664]{1,0:T(8,128)(2,1)}) custom-call(bf16[224,4992]{1,0:T(8,128)(2,1)} %collective-permute-done.2.left_ref, bf16[224,4992]{1,0:T(8,128)(2,1)} %copy-done.2, bf16[224,4992]{1,0:T(8,128)(2,1)} %collective-permute-done.3.right_ref, ...), custom_call_target="tpu_custom_call" | custom-call | tf_op jit(solution)/shard_map/attend_back/pallas_call | solution.py:365
  (78 shorter events, 40.2 us)
Async XLA Ops:
  7.2 133.6 %copy-start = (bf16[1,1664,512]{2,1,0:T(8,128)(2,1)S(1)}, bf16[1,1664,512]{2,1,0:T(8,128)(2,1)}, u32[]{:S(2)}) copy-start(bf16[1,1664,512]{2,1,0:T(8,128)(2,1)} %param.18) | copy-start | bytes 5111812
  7.2 75.6 %all-gather.3.cloned.1.call-start = ((), (), s32[]{:S(2)}) async-start(), calls=%async_computation.4 | async-start | bytes 5750784 | tf_op jit(solution)/shard_map/all_gather | solution.py:333
  8.8 40.5 %copy-start.3 = (bf16[16,8,1664]{2,1,0:T(8,128)(2,1)S(1)}, bf16[16,8,1664]{2,1,0:T(8,128)(2,1)}, u32[]{:S(2)}) copy-start(bf16[16,8,1664]{2,1,0:T(8,128)(2,1)} %param.13) | copy-start | bytes 1277956
  11.2 38.8 %copy-start.10 = (f32[1664]{0:T(1024)S(1)}, f32[1664]{0:T(1024)}, u32[]{:S(2)}) copy-start(f32[1664]{0:T(1024)} %param.15) | copy-start | bytes 19972
  49.3 73.9 %all-gather.5.cloned.1.call-start = ((), (), s32[]{:S(2)}) async-start(), calls=%async_computation.5 | async-start | bytes 5750784 | tf_op jit(solution)/shard_map/all_gather | solution.py:332
  82.2 124.4 %reduce-scatter.2.cloned.1.call-start = ((), (), s32[]{:S(2)}) async-start(), calls=%async_computation.6 | async-start | bytes 5750784 | tf_op jit(solution)/shard_map/reduce_scatter | solution.py:338
  140.8 5.0 %copy-start.11 = (bf16[1,512,1664]{2,1,0:T(8,128)(2,1)S(1)}, bf16[1,512,1664]{2,1,0:T(8,128)(2,1)}, u32[]{:S(2)}) copy-start(bf16[1,512,1664]{2,1,0:T(8,128)(2,1)} %param.19) | copy-start | bytes 5111812
  145.8 7.5 %copy-start.14 = (f32[1536,512]{1,0:T(8,128)}, f32[1536,512]{1,0:T(8,128)S(1)}, u32[]{:S(2)}) copy-start(f32[1536,512]{1,0:T(8,128)S(1)} %fusion.8) | copy-start | bytes 9437188
  160.6 14.1 %collective-permute-start = (bf16[48,4992]{1,0:T(8,128)(2,1)S(1)}, bf16[48,4992]{1,0:T(8,128)(2,1)S(1)}, u32[]{:S(2)}, u32[]{:S(2)}) collective-permute-start(bf16[48,4992]{1,0:T(8,128)(2,1)S(1)} %get-tuple-element.20), channel_id=1, source_target_pairs={{0,1},{1,2},{2,3},{3,4},{4,5},{5,6},{6,7},{7,8},{8,9},{9,10},{10,1... | collective-permute-start | bytes 1437704 | tf_op jit(solution)/shard_map/ppermute | solution.py:268
  164.1 14.7 %collective-permute-start.1 = (bf16[48,4992]{1,0:T(8,128)(2,1)S(1)}, bf16[48,4992]{1,0:T(8,128)(2,1)S(1)}, u32[]{:S(2)}, u32[]{:S(2)}) collective-permute-start(bf16[48,4992]{1,0:T(8,128)(2,1)S(1)} %get-tuple-element.21), channel_id=1, source_target_pairs={{1,0},{2,1},{3,2},{4,3},{5,4},{6,5},{7,6},{8,7},{9,8},{10,9},{11,1... | collective-permute-start | bytes 1437704 | tf_op jit(solution)/shard_map/ppermute | solution.py:269
  185.2 46.1 %copy-start.2 = (bf16[224,4992]{1,0:T(8,128)(2,1)}, bf16[224,4992]{1,0:T(8,128)(2,1)S(1)}, u32[]{:S(2)}) copy-start(bf16[224,4992]{1,0:T(8,128)(2,1)S(1)} %pad_maximum_fusion.mid_ref) | copy-start | bytes 6709252
  185.2 35.7 %collective-permute-start.3 = (bf16[224,4992]{1,0:T(8,128)(2,1)S(1)}, bf16[224,4992]{1,0:T(8,128)(2,1)}, u32[]{:S(2)}, u32[]{:S(2)}) collective-permute-start(bf16[224,4992]{1,0:T(8,128)(2,1)S(1)} %pad_maximum_fusion.mid_ref), channel_id=1, source_target_pairs={{32,0},{64,32},{96,64},{128,96},{160,128},{192,160},{224,192},{33,... | collective-permute-start | bytes 6709256 | tf_op jit(solution)/shard_map/ppermute | solution.py:273
  187.4 34.8 %collective-permute-start.2 = (bf16[224,4992]{1,0:T(8,128)(2,1)S(1)}, bf16[224,4992]{1,0:T(8,128)(2,1)}, u32[]{:S(2)}, u32[]{:S(2)}) collective-permute-start(bf16[224,4992]{1,0:T(8,128)(2,1)S(1)} %pad_maximum_fusion.mid_ref), channel_id=1, source_target_pairs={{0,32},{32,64},{64,96},{96,128},{128,160},{160,192},{192,224},{1,3... | collective-permute-start | bytes 6709256 | tf_op jit(solution)/shard_map/ppermute | solution.py:272
  208.7 30.3 %all-to-all-start.2 = ((bf16[32,6,1664]{2,1,0:T(8,128)(2,1)}), bf16[32,6,1664]{2,1,0:T(8,128)(2,1)}, u32[]{:S(2)}, u32[]{:S(2)}) async-start(bf16[32,6,1664]{2,1,0:T(8,128)(2,1)} %reshape.121), calls=%async_computation.3 | async-start | bytes 1703936 | tf_op jit(solution)/shard_map/all_to_all | solution.py:344
  232.3 8.5 %copy-start.5 = (bf16[16,8,1664]{2,1,0:T(8,128)(2,1)S(1)}, bf16[16,8,1664]{2,1,0:T(8,128)(2,1)}, u32[]{:S(2)}) copy-start(bf16[16,8,1664]{2,1,0:T(8,128)(2,1)} %param.14) | copy-start | bytes 1277956
  240.4 6.6 %copy-start.13 = (bf16[1536,512]{1,0:T(8,128)(2,1)S(1)}, bf16[1536,512]{1,0:T(8,128)(2,1)}, u32[]{:S(2)}) copy-start(bf16[1536,512]{1,0:T(8,128)(2,1)} %copy-done.12) | copy-start | bytes 4718596
  242.8 28.6 %slice-start = ((s8[5111808]{0:T(1024)(128)(4,1)}), s8[4194304]{0:T(1024)(128)(4,1)S(1)}, s32[]{:S(2)}) async-start(s8[5111808]{0:T(1024)(128)(4,1)} %bitcast.46), calls=%async_computation.7 | async-start | bytes 8388608
  242.8 28.6 %slice-start.1 = ((s8[5111808]{0:T(1024)(128)(4,1)}), s8[917504]{0:T(1024)(128)(4,1)S(1)}, s32[]{:S(2)}) async-start(s8[5111808]{0:T(1024)(128)(4,1)} %bitcast.46), calls=%async_computation.8 | async-start | bytes 1835008
  242.9 28.6 %copy-start.15 = (f32[1536,512]{1,0:T(8,128)S(1)}, f32[1536,512]{1,0:T(8,128)}, u32[]{:S(2)}) copy-start(f32[1536,512]{1,0:T(8,128)} %copy-done.14) | copy-start | bytes 9437188
  242.9 12.0 %collective-permute-start.4 = (bf16[48,1792]{1,0:T(8,128)(2,1)S(1)}, bf16[48,1792]{1,0:T(8,128)(2,1)S(1)}, u32[]{:S(2)}, u32[]{:S(2)}) collective-permute-start(bf16[48,1792]{1,0:T(8,128)(2,1)S(1)} %get-tuple-element.23), channel_id=1, source_target_pairs={{0,1},{1,2},{2,3},{3,4},{4,5},{5,6},{6,7},{7,8},{8,9},{9,10},{10,1... | collective-permute-start | bytes 516104 | tf_op jit(solution)/shard_map/ppermute | solution.py:268
  253.5 7.3 %collective-permute-start.5 = (bf16[48,1792]{1,0:T(8,128)(2,1)S(1)}, bf16[48,1792]{1,0:T(8,128)(2,1)S(1)}, u32[]{:S(2)}, u32[]{:S(2)}) collective-permute-start(bf16[48,1792]{1,0:T(8,128)(2,1)S(1)} %get-tuple-element.22), channel_id=1, source_target_pairs={{1,0},{2,1},{3,2},{4,3},{5,4},{6,5},{7,6},{8,7},{9,8},{10,9},{11,1... | collective-permute-start | bytes 516104 | tf_op jit(solution)/shard_map/ppermute | solution.py:269
  260.8 18.2 %collective-permute-start.7 = (bf16[224,1792]{1,0:T(8,128)(2,1)S(1)}, bf16[224,1792]{1,0:T(8,128)(2,1)S(1)}, u32[]{:S(2)}, u32[]{:S(2)}) collective-permute-start(bf16[224,1792]{1,0:T(8,128)(2,1)S(1)} %constant_dynamic-update-slice_fusion.gmid_ref), channel_id=1, source_target_pairs={{32,0},{64,32},{96,64},{128,96},{160,128},{192,160},{224,192},{33,... | collective-permute-start | bytes 2408456 | tf_op jit(solution)/shard_map/ppermute | solution.py:273
  269.3 13.5 %collective-permute-start.6 = (bf16[224,1792]{1,0:T(8,128)(2,1)S(1)}, bf16[224,1792]{1,0:T(8,128)(2,1)S(1)}, u32[]{:S(2)}, u32[]{:S(2)}) collective-permute-start(bf16[224,1792]{1,0:T(8,128)(2,1)S(1)} %constant_dynamic-update-slice_fusion.gmid_ref), channel_id=1, source_target_pairs={{0,32},{32,64},{64,96},{96,128},{128,160},{160,192},{192,224},{1,3... | collective-permute-start | bytes 2408456 | tf_op jit(solution)/shard_map/ppermute | solution.py:272
  271.5 27.0 %copy-start.1 = (bf16[1,1664,512]{2,1,0:T(8,128)(2,1)S(1)}, bf16[1,1664,512]{2,1,0:T(8,128)(2,1)}, u32[]{:S(2)}) copy-start(bf16[1,1664,512]{2,1,0:T(8,128)(2,1)} %param.18) | copy-start | bytes 5111812
  (6 other events, 7.2 us)
Sparse Core Ops, SparseCore 0:
  49.4 32.7 all-gather.2
  84.6 38.5 all-gather.4
  159.4 47.1 reduce-scatter.1

commit v2 on v1

--- a/solution.py
+++ b/solution.py
@@ -9,6 +9,8 @@
 
 HEADS = 16
 RAD = 6
+SLOTS = 6
+MESH = pl.DeviceIdType.MESH
 VMEM_LIMIT = 48 * 1024 * 1024
 
 
@@ -62,16 +64,473 @@
     return (grad_first.astype(jnp.bfloat16), grad_second.astype(jnp.bfloat16), back_terms)
 
 
-def dispatch_table(routes, experts, capacity):
-    tokens = routes.shape[0]
-    onehot = (routes[:, None] == jnp.arange(experts, dtype=jnp.int32)[None, :]).astype(jnp.bfloat16)
-    earlier = (jnp.arange(tokens)[:, None] > jnp.arange(tokens)[None, :]).astype(jnp.bfloat16)
-    before = jnp.dot(earlier, onehot, preferred_element_type=jnp.float32)
-    ranks = jnp.sum(before * onehot.astype(jnp.float32), axis=1).astype(jnp.int32)
-    target = routes * capacity + ranks
-    return (jnp.arange(experts * capacity, dtype=jnp.int32)[:, None] == target[None, :]).astype(
+def unit_places(index, first):
+    place = index % 16
+    block = index // 16
+    rank = place - first
+    return jnp.where((rank >= 0) & (rank < SLOTS), block * SLOTS + rank, -1)
+
+
+def slot_rows(index):
+    place = index % 16
+    block = index // 16
+    tail = jnp.where(place >= 12, block * SLOTS + place - 12, -1)
+    late = jnp.where((place == 12) | (place == 13), block * SLOTS + place - 8, -1)
+    last = jnp.where(place >= 14, block * SLOTS + place - 10, -1)
+    return (unit_places(index, 0), unit_places(index, 6), tail, late, last)
+
+
+def pack_tables(slots, rows):
+    index = lax.broadcasted_iota(jnp.int32, (rows, 1), 0)
+    return [jnp.where(held == slots, 1.0, 0.0).astype(jnp.bfloat16) for held in slot_rows(index)]
+
+
+def unpack_tables(slots, rows):
+    index = lax.broadcasted_iota(jnp.int32, (1, rows), 1)
+    return [jnp.where(held == slots, 1.0, 0.0).astype(jnp.bfloat16) for held in slot_rows(index)]
+
+
+def pack_rows(tables, values):
+    t0, t1, t2, t3, t4 = tables
+    chunk = [values[:, 128 * i : 128 * (i + 1)] for i in range(10, 13)]
+    tail = jnp.concatenate(
+        [
+            nn_dot(t2, values[:, 1280:1664]),
+            nn_dot(t3, chunk[0]) + nn_dot(t4, chunk[1]),
+            nn_dot(t3, chunk[2]),
+        ],
+        axis=1,
+    )
+    return (nn_dot(t0, values[:, :640]) + nn_dot(t1, values[:, 640:1280]) + tail).astype(
         jnp.bfloat16
     )
+
+
+def unpack_rows(tables, packed):
+    t0, t1, t2, t3, t4 = tables
+    third, fourth = packed[:, 384:512], packed[:, 512:640]
+    extra = jnp.concatenate([nn_dot(t3, third), nn_dot(t4, third), nn_dot(t3, fourth)], axis=1)
+    return jnp.concatenate(
+        [nn_dot(t0, packed), nn_dot(t1, packed), nn_dot(t2, packed[:, :384]) + extra], axis=1
+    )
+
+
+def as_column(row):
+    count = row.shape[1]
+    diagonal = lax.broadcasted_iota(jnp.int32, (count, count), 0) == lax.broadcasted_iota(
+        jnp.int32, (count, count), 1
+    )
+    return jnp.sum(jnp.where(diagonal, row, 0.0), axis=1, keepdims=True)
+
+
+def slot_numbers(routes):
+    tokens = routes.shape[1]
+    onehot = lax.broadcasted_iota(jnp.int32, (128, tokens), 0) == routes
+    onehot = jnp.where(onehot, 1.0, 0.0)
+    earlier = lax.broadcasted_iota(jnp.int32, (tokens, tokens), 0) < lax.broadcasted_iota(
+        jnp.int32, (tokens, tokens), 1
+    )
+    before = nn_dot(
+        onehot.astype(jnp.bfloat16), jnp.where(earlier, 1.0, 0.0).astype(jnp.bfloat16)
+    )
+    rank = jnp.sum(before * onehot, axis=0, keepdims=True)
+    return routes.astype(jnp.float32) * SLOTS + rank
+
+
+def message_kernel(stream_ref, grad_ref, gain_ref, gate_ref, route_ref, out_ref):
+    _, _, expert_in = layer_norm(stream_ref[...], gain_ref[...])
+    grad_z = (as_column(gate_ref[...]) * grad_ref[...].astype(jnp.float32)).astype(jnp.bfloat16)
+    slots = slot_numbers(route_ref[...]).astype(jnp.int32)
+    tables = pack_tables(slots, out_ref.shape[0])
+    out_ref[:, :640] = pack_rows(tables, expert_in)
+    out_ref[:, 640:] = pack_rows(tables, grad_z)
+
+
+def ring_places():
+    e = lax.axis_index("expert")
+    d = lax.axis_index("dp")
+    places = dict(
+        right=lax.rem(e + 2, 8),
+        left=lax.rem(e + 6, 8),
+        far=lax.rem(e + 4, 8),
+        pair=e + 1 - 2 * lax.rem(e, 2),
+    )
+    return e, d, d // 8, lax.rem(d, 8), places
+
+
+def greet_all(d, places):
+    barrier = pltpu.get_barrier_semaphore()
+
+    def greet(i, carry):
+        pl.semaphore_signal(
+            barrier, inc=1, device_id={"dp": lax.rem(d + i, 32)}, device_id_type=MESH
+        )
+        return carry
+
+    lax.fori_loop(1, 32, greet, 0)
+    for name in ("right", "left", "pair"):
+        pl.semaphore_signal(
+            barrier, inc=1, device_id={"expert": places[name]}, device_id_type=MESH
+        )
+    pl.semaphore_wait(barrier, 34)
+
+
+def remote(src, dst, send, recv, **where):
+    return pltpu.make_async_remote_copy(
+        src_ref=src, dst_ref=dst, send_sem=send, recv_sem=recv, device_id=where, device_id_type=MESH
+    )
+
+
+def dispatch_kernel(
+    msg_ref,
+    key_ref,
+    value_ref,
+    query_ref,
+    bx_ref,
+    bg_ref,
+    mid_ref,
+    recv,
+    stage,
+    all_send,
+    all_recv,
+    own_sem,
+    ring_recv,
+    ring_send,
+    keep_sem,
+    rim_send,
+    rim_recv,
+    rim_keep,
+):
+    e, d, x, z, places = ring_places()
+    width = key_ref.shape[1]
+    boxes = (bx_ref, bg_ref)
+    greet_all(d, places)
+
+    def message(target):
+        return remote(
+            msg_ref.at[target],
+            recv.at[x, pl.ds(pl.multiple_of(z * 16, 16), 16)],
+            all_send.at[target],
+            all_recv.at[d],
+            dp=target,
+        )
+
+    own = pltpu.make_async_copy(
+        msg_ref.at[d], recv.at[x, pl.ds(pl.multiple_of(z * 16, 16), 16)], own_sem
+    )
+    own.start()
+    for g in range(4):
+        row = lax.rem(x + g, 4) * 8
+
+        def send(i, carry):
+            message(row + lax.rem(z + i, 8)).start()
+            return carry
+
+        lax.fori_loop(1 if g == 0 else 0, 8, send, 0)
+
+    rim = 48
+    tokens = key_ref.shape[0]
+    after, before = lax.rem(d + 1, 32), lax.rem(d + 31, 32)
+    rims, keeps = [], []
+    for i, ref in enumerate((key_ref, value_ref, query_ref)):
+        lanes = pl.ds(i * width, width)
+        rims.append(
+            remote(
+                ref.at[pl.ds(tokens - rim, rim)],
+                mid_ref.at[pl.ds(0, rim), lanes],
+                rim_send.at[i, 0],
+                rim_recv.at[i, 0],
+                dp=after,
+            )
+        )
+        rims.append(
+            remote(
+                ref.at[pl.ds(0, rim)],
+                mid_ref.at[pl.ds(tokens + rim, rim), lanes],
+                rim_send.at[i, 1],
+                rim_recv.at[i, 1],
+                dp=before,
+            )
+        )
+        keeps.append(
+            pltpu.make_async_copy(ref, mid_ref.at[pl.ds(rim, tokens), lanes], rim_keep.at[i])
+        )
+    for copy in rims + keeps:
+        copy.start()
+
+    index = lax.broadcasted_iota(jnp.int32, (8 * SLOTS, 1), 0)
+    tables = unpack_tables(index, 128)
+
+    def group(g):
+        return lax.rem(x + 4 - g, 4)
+
+    def ring(source, g, kind, where, number, staged=False):
+        src = stage.at[g, kind] if staged else boxes[kind].at[source, group(g)]
+        return remote(
+            src,
+            boxes[kind].at[source, group(g)],
+            ring_send.at[g, kind, number],
+            ring_recv.at[source, group(g), kind],
+            expert=places[where],
+        )
+
+    sent = []
+    for g in range(6):
+        if g < 4:
+            row = group(g) * 8
+
+            def take(i, carry):
+                source = row + lax.rem(z + 8 - i, 8)
+                remote(
+                    msg_ref.at[source],
+                    recv.at[group(g), pl.ds(pl.multiple_of(lax.rem(source, 8) * 16, 16), 16)],
+                    all_send.at[source],
+                    all_recv.at[source],
+                    dp=source,
+                ).wait_recv()
+                return carry
+
+            lax.fori_loop(1 if g == 0 else 0, 8, take, 0)
+            if g == 0:
+                own.wait()
+            for kind in range(2):
+                got = recv[group(g), :, 640 * kind : 640 * (kind + 1)]
+                stage[g, kind] = unpack_rows(tables, got).astype(jnp.bfloat16)
+                for number, where in enumerate(("right", "left", "pair")):
+                    copy = ring(e, g, kind, where, number, True)
+                    copy.start()
+                    sent.append(copy)
+                copy = pltpu.make_async_copy(
+                    stage.at[g, kind], boxes[kind].at[e, group(g)], keep_sem.at[g, kind]
+                )
+                copy.start()
+        if 1 <= g < 5:
+            h = g - 1
+            for name, onward, passed, number in (("left", "right", 0, 3), ("right", "left", 1, 4)):
+                source = places[name]
+                for kind in range(2):
+                    ring(source, h, kind, "right", 0).wait_recv()
+                    if kind == passed:
+                        copy = ring(source, h, kind, onward, 3)
+                        copy.start()
+                        sent.append(copy)
+                    copy = ring(source, h, kind, "pair", number + 1)
+                    copy.start()
+                    sent.append(copy)
+        if 2 <= g:
+            h = g - 2
+            for kind in range(2):
+                ring(places["far"], h, kind, "right", 0).wait_recv()
+                copy = ring(places["far"], h, kind, "pair", 6)
+                copy.start()
+                sent.append(copy)
+    side = lax.rem(e, 2)
+    for g in range(4):
+        for y in range(4):
+            for kind in range(2):
+                ring(2 * y + 1 - side, g, kind, "right", 0).wait_recv()
+    for copy in sent:
+        copy.wait_send()
+    for g in range(4):
+        for kind in range(2):
+            pltpu.make_async_copy(
+                stage.at[g, kind], boxes[kind].at[e, group(g)], keep_sem.at[g, kind]
+            ).wait()
+
+    def sent_all(i, carry):
+        message(lax.rem(d + i, 32)).wait_send()
+        return carry
+
+    lax.fori_loop(1, 32, sent_all, 0)
+    for copy in rims:
+        copy.wait()
+    for copy in keeps:
+        copy.wait()
+
+
+def return_kernel(
+    back_ref,
+    out_ref,
+    from_pair,
+    mine,
+    from_left,
+    from_right,
+    early,
+    packed,
+    pair_send,
+    pair_recv,
+    far_send,
+    far_recv,
+    near_send,
+    near_recv,
+    all_send,
+    all_recv,
+    own_sem,
+):
+    e, d, x, z, places = ring_places()
+    greet_all(d, places)
+    right, left, far, pair = (places[name] for name in ("right", "left", "far", "pair"))
+
+    def group(g):
+        return lax.rem(x + g, 4)
+
+    order = ((2, far), (1, right), (3, left), (0, e))
+    pairs = []
+    for step, target in order:
+        other = target + pair - e
+        copy = remote(
+            back_ref.at[other],
+            from_pair.at[step],
+            pair_send.at[step],
+            pair_recv.at[step],
+            expert=pair,
+        )
+        copy.start()
+        pairs.append(copy)
+
+    def joined(step, target, g):
+        return back_ref[target, group(g)].astype(jnp.float32) + from_pair[step, group(g)].astype(
+            jnp.float32
+        )
+
+    def far_copy(g):
+        return remote(
+            mine.at[2, g],
+            early.at[g],
+            far_send.at[g],
+            far_recv.at[g],
+            expert=right if g < 2 else left,
+        )
+
+    def near_copy(step, g):
+        return remote(
+            mine.at[step, g],
+            (from_left if step == 1 else from_right).at[g],
+            near_send.at[step // 2, g],
+            near_recv.at[step // 2, g],
+            expert=right if step == 1 else left,
+        )
+
+    pairs[0].wait_recv()
+    for g in (0, 2, 1, 3):
+        mine[2, g] = joined(2, far, g).astype(jnp.bfloat16)
+        far_copy(g).start()
+    pairs[1].wait_recv()
+    for g in (2, 3):
+        mine[1, g] = joined(1, right, g).astype(jnp.bfloat16)
+        near_copy(1, g).start()
+    pairs[2].wait_recv()
+    for g in (0, 1):
+        mine[3, g] = joined(3, left, g).astype(jnp.bfloat16)
+        near_copy(3, g).start()
+    for g in (0, 1):
+        far_copy(g).wait_recv()
+        mine[1, g] = (joined(1, right, g) + early[g].astype(jnp.float32)).astype(jnp.bfloat16)
+        near_copy(1, g).start()
+        far_copy(g + 2).wait_recv()
+        mine[3, g + 2] = (joined(3, left, g + 2) + early[g + 2].astype(jnp.float32)).astype(
+            jnp.bfloat16
+        )
+        near_copy(3, g + 2).start()
+    pairs[3].wait_recv()
+    index = lax.broadcasted_iota(jnp.int32, (1, 8 * SLOTS), 1)
+    tables = pack_tables(index, 128)
+
+    def message(g, i):
+        place = lax.rem(z + i, 8)
+        target = group(g) * 8 + place
+        rows = pl.ds(pl.multiple_of(place * 16, 16), 16)
+        return remote(
+            packed.at[g, rows], out_ref.at[d], all_send.at[target], all_recv.at[d], dp=target
+        )
+
+    own = pltpu.make_async_copy(
+        packed.at[0, pl.ds(pl.multiple_of(z * 16, 16), 16)], out_ref.at[d], own_sem
+    )
+    for g in (0, 2, 1, 3):
+        near_copy(1, g).wait_recv()
+        near_copy(3, g).wait_recv()
+        total = (
+            joined(0, e, g)
+            + from_left[g].astype(jnp.float32)
+            + from_right[g].astype(jnp.float32)
+        )
+        packed[g] = pack_rows(tables, total.astype(jnp.bfloat16))
+
+        def send(i, carry):
+            message(g, i).start()
+            return carry
+
+        lax.fori_loop(1 if g == 0 else 0, 8, send, 0)
+        if g == 0:
+            own.start()
+
+    def take(i, carry):
+        source = lax.rem(d + i, 32)
+        remote(
+            packed.at[0, pl.ds(0, 16)],
+            out_ref.at[source],
+            all_send.at[source],
+            all_recv.at[source],
+            dp=source,
+        ).wait_recv()
+        return carry
+
+    lax.fori_loop(1, 32, take, 0)
+    own.wait()
+    for copy in pairs:
+        copy.wait_send()
+    for g in range(4):
+        far_copy(g).wait_send()
+        near_copy(1, g).wait_send()
+        near_copy(3, g).wait_send()
+        lax.fori_loop(
+            1 if g == 0 else 0, 8, lambda i, carry: (message(g, i).wait_send(), carry)[1], 0
+        )
+
+
+def halo_kernel(block_ref, left_ref, mid_ref, right_ref, send_sem, recv_sem, own_sem):
+    e = lax.axis_index("expert")
+    d = lax.axis_index("dp")
+    tokens = block_ref.shape[0]
+    rim = (left_ref.shape[0] - tokens) // 2
+    places = []
+    for down in (-1, 0, 1):
+        for over in (-1, 0, 1):
+            if down or over:
+                places.append((down, over, lax.rem(d + 32 + down, 32), lax.rem(e + 8 + over, 8)))
+    barrier = pltpu.get_barrier_semaphore()
+    for _, _, row, col in places:
+        pl.semaphore_signal(
+            barrier, inc=1, device_id={"dp": row, "expert": col}, device_id_type=MESH
+        )
+    pl.semaphore_wait(barrier, len(places))
+    own = pltpu.make_async_copy(block_ref, mid_ref.at[pl.ds(rim, tokens)], own_sem)
+    copies = []
+    for number, (down, over, row, col) in enumerate(places):
+        side = {1: left_ref, 0: mid_ref, -1: right_ref}[over]
+        if down == 0:
+            src, dst = pl.ds(0, tokens), pl.ds(rim, tokens)
+        elif down == 1:
+            src, dst = pl.ds(tokens - rim, rim), pl.ds(0, rim)
+        else:
+            src, dst = pl.ds(0, rim), pl.ds(rim + tokens, rim)
+        copies.append(
+            remote(
+                block_ref.at[src],
+                side.at[dst],
+                send_sem.at[number],
+                recv_sem.at[number],
+                dp=row,
+                expert=col,
+            )
+        )
+    for number in (3, 4, 0, 2, 5, 7, 1, 6):
+        copies[number].start()
+    own.start()
+    for copy in copies:
+        copy.wait()
+    own.wait()
 
 
 def head_lanes(head, size, width):
@@ -157,13 +616,17 @@
     return first, second, third
 
 
-def stream_kernel(stream_ref, grad_ref, gain_ref, back_ref, att_ref, stats_ref, plain_ref, packed_ref):
+def stream_kernel(
+    stream_ref, grad_ref, gain_ref, route_ref, back_ref, att_ref, stats_ref, plain_ref, packed_ref
+):
     width = stream_ref.shape[1]
     size = width // HEADS
     gain = gain_ref[...]
     normed, inv_std, _ = layer_norm(stream_ref[...], gain)
+    slots = as_column(slot_numbers(route_ref[...])).astype(jnp.int32)
+    grad_in = unpack_rows(unpack_tables(slots, back_ref.shape[0]), back_ref[...])
     grad_stream = (
-        grad_ref[...].astype(jnp.float32) + norm_backward(back_ref[...], normed, inv_std, gain)
+        grad_ref[...].astype(jnp.float32) + norm_backward(grad_in, normed, inv_std, gain)
     ).astype(jnp.bfloat16)
     plain_ref[...] = grad_stream
     packed_ref[:, :width] = grad_stream
@@ -258,20 +721,28 @@
     return pl.BlockSpec(memory_space=pltpu.VMEM)
 
 
-def wide_halo(block, rim):
-    def pairs(axis):
-        count = lax.axis_size(axis)
-        forward = [(i, i + 1) for i in range(count - 1)]
-        return forward, [(b, a) for a, b in forward]
-
-    forward, backward = pairs("dp")
-    upper = lax.ppermute(block[block.shape[0] - rim :], "dp", forward)
-    lower = lax.ppermute(block[:rim], "dp", backward)
-    mid = jnp.concatenate([upper, block, lower], axis=0)
-    forward, backward = pairs("expert")
-    left = lax.ppermute(mid, "expert", forward)
-    right = lax.ppermute(mid, "expert", backward)
-    return left, mid, right
+def sides(mid):
+    count = lax.axis_size("expert")
+    forward = [(i, i + 1) for i in range(count - 1)]
+    backward = [(b, a) for a, b in forward]
+    return lax.ppermute(mid, "expert", forward), mid, lax.ppermute(mid, "expert", backward)
+
+
+def anywhere():
+    return pl.BlockSpec(memory_space=pl.ANY)
+
+
+def params(collective_id=None):
+    if collective_id is None:
+        return pltpu.CompilerParams(vmem_limit_bytes=VMEM_LIMIT)
+    return pltpu.CompilerParams(
+        vmem_limit_bytes=VMEM_LIMIT, collective_id=collective_id, has_side_effects=True
+    )
+
+
+def shaped(shape, kind=jnp.bfloat16):
+    return jax.ShapeDtypeStruct(shape, kind)
+
 
 def body(
     query_act,
@@ -289,87 +760,107 @@
     tokens = band * cols
     experts = lax.axis_size("dp")
     col_parts = lax.axis_size("expert")
-    capacity = max(2, tokens * 3 // (2 * experts))
     sizes = (band, cols, band * experts, cols * col_parts)
     side = (band + 2 * RAD) * cols
-    flat_query = query_act.reshape(tokens, width)
-    joined = jnp.concatenate(
-        [key_act.reshape(tokens, width), value_act.reshape(tokens, width), flat_query], axis=-1
-    )
-    near = wide_halo(joined, RAD * cols)
+    dma = pltpu.SemaphoreType.DMA
+    flat_query, flat_key, flat_value, flat_stream, flat_grad = (
+        array.reshape(tokens, width) for array in (query_act, key_act, value_act, stream, grad_out)
+    )
+    gain = norm_gain.reshape(1, width)
+    routes = route_ids.reshape(1, tokens)
+    messages = pl.pallas_call(
+        message_kernel,
+        out_shape=shaped((experts * 16, 1280)),
+        in_specs=[vmem()] * 5,
+        out_specs=vmem(),
+        compiler_params=params(),
+        name="messages",
+    )(flat_stream, flat_grad, gain, gate_prob.reshape(1, tokens), routes)
+    rows_in, rows_grad, mid = pl.pallas_call(
+        dispatch_kernel,
+        out_shape=(
+            shaped((8, 4, 48, width)),
+            shaped((8, 4, 48, width)),
+            shaped((side, 3 * width)),
+        ),
+        in_specs=[vmem()] + [anywhere()] * 3,
+        out_specs=(anywhere(),) * 3,
+        scratch_shapes=[
+            pltpu.VMEM((4, 128, 1280), jnp.bfloat16),
+            pltpu.VMEM((4, 2, 48, width), jnp.bfloat16),
+            dma((32,)),
+            dma((32,)),
+            dma,
+            dma((8, 4, 2)),
+            dma((4, 2, 7)),
+            dma((4, 2)),
+            dma((3, 2)),
+            dma((3, 2)),
+            dma((3,)),
+        ],
+        compiler_params=params(1),
+        name="dispatch",
+    )(messages.reshape(experts, 16, 1280), flat_key, flat_value, flat_query)
+    near = sides(mid)
+    grad_first, grad_second, back_terms = expert_grads(
+        rows_in.reshape(-1, width), rows_grad.reshape(-1, width), weight_in[0], weight_out[0]
+    )
     attended, log_total = pl.pallas_call(
         functools.partial(forward_kernel, sizes),
-        out_shape=(
-            jax.ShapeDtypeStruct((tokens, width), jnp.float32),
-            jax.ShapeDtypeStruct((tokens, 128), jnp.float32),
-        ),
+        out_shape=(shaped((tokens, width), jnp.float32), shaped((tokens, 128), jnp.float32)),
         in_specs=[vmem()] * 4,
         out_specs=(vmem(), vmem()),
         scratch_shapes=[pltpu.VMEM((tokens, 3 * side), jnp.float32)],
-        compiler_params=pltpu.CompilerParams(vmem_limit_bytes=VMEM_LIMIT),
+        compiler_params=params(),
         name="attend",
     )(flat_query, *near)
-    flat_stream = stream.reshape(tokens, width)
-    flat_grad = grad_out.reshape(tokens, width)
-    normed, inv_std, expert_in = layer_norm(flat_stream, norm_gain)
-    grad_z = (gate_prob.reshape(tokens, 1) * flat_grad.astype(jnp.float32)).astype(jnp.bfloat16)
-    table = dispatch_table(route_ids.reshape(tokens), experts, capacity)
-    slots_in = (
-        jnp.dot(table, expert_in, preferred_element_type=jnp.float32)
-        .astype(jnp.bfloat16)
-        .reshape(experts, capacity, width)
-    )
-    slots_grad = (
-        jnp.dot(table, grad_z, preferred_element_type=jnp.float32)
-        .astype(jnp.bfloat16)
-        .reshape(experts, capacity, width)
-    )
-    arrived_in, arrived_grad = (
-        lax.all_to_all(slots_in, "dp", split_axis=0, concat_axis=0, tiled=True),
-        lax.all_to_all(slots_grad, "dp", split_axis=0, concat_axis=0, tiled=True),
-    )
-    rows_in, rows_grad = (
-        lax.all_gather(arrived_in, "expert", axis=0, tiled=True),
-        lax.all_gather(arrived_grad, "expert", axis=0, tiled=True),
-    )
-    grad_first, grad_second, back_terms = expert_grads(
-        rows_in.reshape(-1, width), rows_grad.reshape(-1, width), weight_in[0], weight_out[0]
-    )
-    own_terms = lax.psum_scatter(
-        back_terms.reshape(col_parts, experts * capacity, width).astype(jnp.bfloat16),
-        "expert",
-        scatter_dimension=0,
-        tiled=True,
-    )
-    returned = lax.all_to_all(
-        own_terms.reshape(experts, capacity, width), "dp", split_axis=0, concat_axis=0, tiled=True
-    )
-    grad_u = lax.dot_general(
-        table,
-        returned.reshape(experts * capacity, width),
-        (((0,), (0,)), ((), ())),
-        preferred_element_type=jnp.float32,
-    )
+    returned = pl.pallas_call(
+        return_kernel,
+        out_shape=shaped((experts, 16, 640)),
+        in_specs=[vmem()],
+        out_specs=vmem(),
+        scratch_shapes=[pltpu.VMEM((4, 4, 48, width), jnp.bfloat16)] * 2
+        + [pltpu.VMEM((4, 48, width), jnp.bfloat16)] * 3
+        + [
+            pltpu.VMEM((4, 128, 640), jnp.bfloat16),
+            dma((4,)),
+            dma((4,)),
+            dma((4,)),
+            dma((4,)),
+            dma((2, 4)),
+            dma((2, 4)),
+            dma((32,)),
+            dma((32,)),
+            dma,
+        ],
+        compiler_params=params(2),
+        name="give_back",
+    )(back_terms.astype(jnp.bfloat16).reshape(8, 4, 48, width))
     plain, packed = pl.pallas_call(
         stream_kernel,
-        out_shape=(
-            jax.ShapeDtypeStruct((tokens, width), jnp.bfloat16),
-            jax.ShapeDtypeStruct((tokens, width + 128), jnp.bfloat16),
-        ),
-        in_specs=[vmem()] * 6,
+        out_shape=(shaped((tokens, width)), shaped((tokens, width + 128))),
+        in_specs=[vmem()] * 7,
         out_specs=(vmem(), vmem()),
-        compiler_params=pltpu.CompilerParams(vmem_limit_bytes=VMEM_LIMIT),
+        compiler_params=params(),
         name="stream_grad",
-    )(flat_stream, flat_grad, norm_gain.reshape(1, width), grad_u, attended, log_total)
-    far = wide_halo(packed, RAD * cols)
+    )(flat_stream, flat_grad, gain, routes, returned.reshape(-1, 640), attended, log_total)
+    far = pl.pallas_call(
+        halo_kernel,
+        out_shape=(shaped((side, width + 128)),) * 3,
+        in_specs=[vmem()],
+        out_specs=(vmem(),) * 3,
+        scratch_shapes=[dma((8,)), dma((8,)), dma],
+        compiler_params=params(3),
+        name="halo",
+    )(packed)
     grad_query, grad_key, grad_value = pl.pallas_call(
         functools.partial(backward_kernel, sizes),
-        out_shape=(jax.ShapeDtypeStruct((tokens, width), jnp.bfloat16),) * 3,
+        out_shape=(shaped((tokens, width)),) * 3,
         in_specs=[vmem()] * 6,
         out_specs=(vmem(),) * 3,
         scratch_shapes=[pltpu.VMEM((tokens, 3 * side), jnp.float32)]
         + [pltpu.VMEM((tokens, width), jnp.float32)] * 3,
-        compiler_params=pltpu.CompilerParams(vmem_limit_bytes=VMEM_LIMIT),
+        compiler_params=params(),
         name="attend_back",
     )(*near, *far)
     shape = (band, cols, width)

time: 309 us -> 196 us (0.63)
  the two profiles are of different devices: /device:TPU:24 before, /device:TPU:10 now
where the time goes in v2:
time: 196 us; the launch traced here: 194 us
  Pallas kernels  158 us (81%)
  matrix products  23.1 us (12%)
  local copies, waits for them, and re-layouts  7.23 us (4%)
  starting transfers between devices  4.93 us (3%)
    pallas_call x1, Pallas kernels, body(): pl.pallas_call(dispatch_kernel, out_shape=(shaped((8, 4, 48, width)), sha...  66.5 us
    pallas_call x1, Pallas kernels, body(): pl.pallas_call(return_kernel, out_shape=shaped((experts, 16, 640)), in_sp...  44.3 us
    pallas_call x1, Pallas kernels, body(): pl.pallas_call(halo_kernel, out_shape=(shaped((side, width + 128)),) * 3,...  19.7 us
    pallas_call x1, Pallas kernels, body(): pl.pallas_call(functools.partial(backward_kernel, sizes), out_shape=(shap...  15 us
    pallas_call x1, Pallas kernels, body(): pl.pallas_call(functools.partial(forward_kernel, sizes), out_shape=(shape...  8.51 us
    dot_general x1, matrix products, expert_grads(): lax.dot_general(rows_in, grad_pre, (((0,), (0,)), ((), ())), preferred_el...  6.61 us
    unnamed x38, local copies, waits for them, and re-layouts  6.4 us
    dot_general x1, matrix products, expert_grads(): pre_act = jnp.dot(rows_in, w_first, preferred_element_type=jnp.float32)  5.05 us
  transfers between devices with their start and end apart: 2, of which 0 were waited for; matrix products, arithmetic and copies ran while one was open for 12% of the time, Pallas kernels for 23%

profile of v2, /device:TPU:10, one launch (start us, length us, event | category | flops | bytes accessed | tf_op | source)
XLA Modules:
  0.0 194.2 jit_solution(15359190140861119861)
XLA Ops:
  0.6 0.0 copy-start
  0.6 0.8 reshape.65.gain_ref
  1.5 1.0 copy-done.2
  2.5 1.0 copy-done.4
  3.5 0.7 copy-done.10
  4.1 0.7 copy-done.12
  4.8 1.6 messages.1
  6.4 1.0 copy-done.6
  7.4 1.0 copy-done.8
  8.4 1.0 copy-done.9
  9.4 66.5 %dispatch.1 = (bf16[8,4,48,1664]{3,2,1,0:T(8,128)(2,1)}, bf16[8,4,48,1664]{3,2,1,0:T(8,128)(2,1)}, bf16[224,4992]{1,0:T(8,128)(2,1)S(1)}) custom-call(bf16[32,16,1280]{2,1,0:T(8,128)(2,1)S(1)} %bitcast.34, bf16[128,1664]{1,0:T(8,128)(2,1)S(1)} %bitcast.43, bf16[128,1664]{1,0:T(8,128)(2,1)S(1)} %bitcast.44, bf16[128,1664]{1,0:T(8,128)(2,1)S(1)} %bitcast.41), custom_call_target="tpu_custom_call" | custom-call | tf_op jit(solution)/shard_map/dispatch/pallas_call | solution.py:779
  75.9 2.8 %collective-permute-start.1 = (bf16[224,4992]{1,0:T(8,128)(2,1)S(1)}, bf16[224,4992]{1,0:T(8,128)(2,1)}, u32[]{:S(2)}, u32[]{:S(2)}) collective-permute-start(bf16[224,4992]{1,0:T(8,128)(2,1)S(1)} %get-tuple-element.19.mid_ref), channel_id=1, source_target_pairs={{32,0},{64,32},{96,64},{128,96},{160,128},{192,160},{224,192},{33,... | collective-permute-start | bytes 6709256 | tf_op jit(solution)/shard_map/ppermute | solution.py:728
  78.7 2.1 %collective-permute-start = (bf16[224,4992]{1,0:T(8,128)(2,1)S(1)}, bf16[224,4992]{1,0:T(8,128)(2,1)S(1)}, u32[]{:S(2)}, u32[]{:S(2)}) collective-permute-start(bf16[224,4992]{1,0:T(8,128)(2,1)S(1)} %get-tuple-element.19.mid_ref), channel_id=1, source_target_pairs={{0,32},{32,64},{64,96},{96,128},{128,160},{160,192},{192,224},{1,3... | collective-permute-start | bytes 6709256 | tf_op jit(solution)/shard_map/ppermute | solution.py:728
  80.9 5.0 %fusion.8 = f32[1536,512]{1,0:T(8,128)S(1)} fusion(bf16[1536,1664]{1,0:T(8,128)(2,1)} %bitcast.52, bf16[1,1664,512]{2,1,0:T(8,128)(2,1)S(1)} %copy-done), kind=kOutput, calls=%fused_computation.15 | convolution fusion | flops 2617245696 | bytes 9961472 | tf_op jit(solution)/shard_map/dot_general | solution.py:49
  86.0 3.9 %fusion.4 = bf16[1536,512]{1,0:T(8,128)(2,1)S(1)} fusion(f32[1536,512]{1,0:T(8,128)S(1)} %fusion.8, bf16[1536,1664]{1,0:T(8,128)(2,1)S(1)} %bitcast.48, bf16[1,512,1664]{2,1,0:T(8,128)(2,1)S(1)} %copy-done.14), kind=kOutput, calls=%fused_computation.9 | convolution fusion | flops 2625110016 | bytes 11534336 | tf_op jit(solution)/shard_map/dot_general | solution.py:51
  89.9 3.3 %convolution_convert_fusion = bf16[1536,1664]{1,0:T(8,128)(2,1)S(1)} fusion(bf16[1536,512]{1,0:T(8,128)(2,1)S(1)} %fusion.4, bf16[1,1664,512]{2,1,0:T(8,128)(2,1)S(1)} %copy-done), kind=kOutput, calls=%fused_computation | convolution fusion | flops 2619801600 | bytes 8388608 | tf_op jit(solution)/shard_map/dot_general | solution.py:61
  93.2 44.3 %give_back.1 = bf16[32,16,640]{2,1,0:T(8,128)(2,1)S(1)} custom-call(bf16[8,4,48,1664]{3,2,1,0:T(8,128)(2,1)S(1)} %bitcast.35), custom_call_target="tpu_custom_call" | custom-call | tf_op jit(solution)/shard_map/give_back/pallas_call | solution.py:817
  137.5 6.6 %fusion.5 = bf16[1,1664,512]{2,1,0:T(8,128)(2,1)} fusion(bf16[1536,1664]{1,0:T(8,128)(2,1)} %bitcast.53, bf16[1536,512]{1,0:T(8,128)(2,1)S(1)} %fusion.4), kind=kOutput, calls=%fused_computation.12 | convolution fusion | flops 2618097664 | bytes 8388608 | tf_op jit(solution)/shard_map/dot_general | solution.py:58
  144.1 0.0 copy-start.7
  144.1 4.3 %fusion.6 = bf16[1,512,1664]{2,1,0:T(8,128)(2,1)} fusion(bf16[1536,1664]{1,0:T(8,128)(2,1)S(1)} %bitcast.51, f32[1536,512]{1,0:T(8,128)S(1)} %copy-done.16), kind=kOutput, calls=%fused_computation.13 | convolution fusion | flops 2622029824 | bytes 9961472 | tf_op jit(solution)/shard_map/dot_general | solution.py:55
  148.4 8.5 %attend.1 = (f32[128,1664]{1,0:T(8,128)S(1)}, f32[128,128]{1,0:T(8,128)S(1)}) custom-call(bf16[128,1664]{1,0:T(8,128)(2,1)S(1)} %bitcast.42, bf16[224,4992]{1,0:T(8,128)(2,1)S(1)} %collective-permute-done.left_ref, bf16[224,4992]{1,0:T(8,128)(2,1)S(1)} %get-tuple-element.19.mid_ref, bf16[224,4992]{1,0:T(8,128)(2,1)} %collective-permute-done.1.right_ref), custom_call_target="tpu_custom_call" | custom-call | tf_op jit(solution)/shard_map/attend/pallas_call | solution.py:808
  157.0 2.5 %stream_grad.1 = (bf16[128,1664]{1,0:T(8,128)(2,1)}, bf16[128,1792]{1,0:T(8,128)(2,1)S(1)}) custom-call(bf16[128,1664]{1,0:T(8,128)(2,1)S(1)} %bitcast.38, bf16[128,1664]{1,0:T(8,128)(2,1)S(1)} %bitcast.40, f32[1,1664]{1,0:T(1,128)S(1)} %reshape.65.gain_ref, s32[1,128]{1,0:T(1,128)S(1)} %bitcast.46, bf16[512,640]{1,0:T(8,128)(2,1)S(1)} %bitcast.36, ...), custom_call_target="tpu_custom_call" | custom-call | tf_op jit(solution)/shard_map/stream_grad/pallas_call | solution.py:839
  159.5 19.7 %halo.1 = (bf16[224,1792]{1,0:T(8,128)(2,1)S(1)}, bf16[224,1792]{1,0:T(8,128)(2,1)S(1)}, bf16[224,1792]{1,0:T(8,128)(2,1)S(1)}) custom-call(bf16[128,1792]{1,0:T(8,128)(2,1)S(1)} %get-tuple-element.24.block_ref), custom_call_target="tpu_custom_call" | custom-call | tf_op jit(solution)/shard_map/halo/pallas_call | solution.py:847
  179.2 15.0 %attend_back.1 = (bf16[128,1664]{1,0:T(8,128)(2,1)}, bf16[128,1664]{1,0:T(8,128)(2,1)}, bf16[128,1664]{1,0:T(8,128)(2,1)}) custom-call(bf16[224,4992]{1,0:T(8,128)(2,1)S(1)} %collective-permute-done.left_ref, bf16[224,4992]{1,0:T(8,128)(2,1)} %copy-done.1, bf16[224,4992]{1,0:T(8,128)(2,1)} %collective-permute-done.1.right_ref, ...), custom_call_target="tpu_custom_call" | custom-call | tf_op jit(solution)/shard_map/attend_back/pallas_call | solution.py:856
  (32 shorter events, 0.1 us)
Async XLA Ops:
  0.6 80.2 %copy-start = (bf16[1,1664,512]{2,1,0:T(8,128)(2,1)S(1)}, bf16[1,1664,512]{2,1,0:T(8,128)(2,1)}, u32[]{:S(2)}) copy-start(bf16[1,1664,512]{2,1,0:T(8,128)(2,1)} %param.18) | copy-start | bytes 5111812
  1.5 1.0 copy-start.2
  2.5 1.0 copy-start.4
  3.5 0.7 copy-start.10
  4.1 0.7 copy-start.12
  6.4 1.0 copy-start.6
  7.4 1.0 copy-start.8
  8.4 1.0 copy-start.9
  75.9 72.6 %copy-start.1 = (bf16[224,4992]{1,0:T(8,128)(2,1)}, bf16[224,4992]{1,0:T(8,128)(2,1)S(1)}, u32[]{:S(2)}) copy-start(bf16[224,4992]{1,0:T(8,128)(2,1)S(1)} %get-tuple-element.19.mid_ref) | copy-start | bytes 6709252
  75.9 72.5 %collective-permute-start.1 = (bf16[224,4992]{1,0:T(8,128)(2,1)S(1)}, bf16[224,4992]{1,0:T(8,128)(2,1)}, u32[]{:S(2)}, u32[]{:S(2)}) collective-permute-start(bf16[224,4992]{1,0:T(8,128)(2,1)S(1)} %get-tuple-element.19.mid_ref), channel_id=1, source_target_pairs={{32,0},{64,32},{96,64},{128,96},{160,128},{192,160},{224,192},{33,... | collective-permute-start | bytes 6709256 | tf_op jit(solution)/shard_map/ppermute | solution.py:728
  78.7 69.7 %collective-permute-start = (bf16[224,4992]{1,0:T(8,128)(2,1)S(1)}, bf16[224,4992]{1,0:T(8,128)(2,1)S(1)}, u32[]{:S(2)}, u32[]{:S(2)}) collective-permute-start(bf16[224,4992]{1,0:T(8,128)(2,1)S(1)} %get-tuple-element.19.mid_ref), channel_id=1, source_target_pairs={{0,32},{32,64},{64,96},{96,128},{128,160},{160,192},{192,224},{1,3... | collective-permute-start | bytes 6709256 | tf_op jit(solution)/shard_map/ppermute | solution.py:728
  80.8 5.1 %copy-start.13 = (bf16[8,4,48,1664]{3,2,1,0:T(8,128)(2,1)S(1)}, bf16[8,4,48,1664]{3,2,1,0:T(8,128)(2,1)}, u32[]{:S(2)}) copy-start(bf16[8,4,48,1664]{3,2,1,0:T(8,128)(2,1)} %get-tuple-element.20) | copy-start | bytes 15335428
  80.9 5.1 %copy-start.14 = (bf16[1,512,1664]{2,1,0:T(8,128)(2,1)S(1)}, bf16[1,512,1664]{2,1,0:T(8,128)(2,1)}, u32[]{:S(2)}) copy-start(bf16[1,512,1664]{2,1,0:T(8,128)(2,1)} %param.19) | copy-start | bytes 5111812
  85.9 4.0 %copy-start.15 = (f32[1536,512]{1,0:T(8,128)}, f32[1536,512]{1,0:T(8,128)S(1)}, u32[]{:S(2)}) copy-start(f32[1536,512]{1,0:T(8,128)S(1)} %fusion.8) | copy-start | bytes 9437188
  93.2 50.9 %slice-start = ((s8[5111808]{0:T(1024)(128)(4,1)}), s8[917504]{0:T(1024)(128)(4,1)S(1)}, s32[]{:S(2)}) async-start(s8[5111808]{0:T(1024)(128)(4,1)} %bitcast.49), calls=%async_computation | async-start | bytes 1835008
  137.5 6.6 %slice-start.1 = ((s8[5111808]{0:T(1024)(128)(4,1)}), s8[4194304]{0:T(1024)(128)(4,1)S(1)}, s32[]{:S(2)}) async-start(s8[5111808]{0:T(1024)(128)(4,1)} %bitcast.49), calls=%async_computation.1 | async-start | bytes 8388608
  137.5 6.6 %copy-start.16 = (f32[1536,512]{1,0:T(8,128)S(1)}, f32[1536,512]{1,0:T(8,128)}, u32[]{:S(2)}) copy-start(f32[1536,512]{1,0:T(8,128)} %copy-done.15) | copy-start | bytes 9437188
  144.1 4.3 %copy-start.7 = (bf16[16,8,1664]{2,1,0:T(8,128)(2,1)S(1)}, bf16[16,8,1664]{2,1,0:T(8,128)(2,1)}, u32[]{:S(2)}) copy-start(bf16[16,8,1664]{2,1,0:T(8,128)(2,1)} %param.10) | copy-start | bytes 1277956
  148.4 8.6 %copy-start.3 = (bf16[16,8,1664]{2,1,0:T(8,128)(2,1)S(1)}, bf16[16,8,1664]{2,1,0:T(8,128)(2,1)}, u32[]{:S(2)}) copy-start(bf16[16,8,1664]{2,1,0:T(8,128)(2,1)} %param.13) | copy-start | bytes 1277956
  148.4 8.6 %copy-start.5 = (bf16[16,8,1664]{2,1,0:T(8,128)(2,1)S(1)}, bf16[16,8,1664]{2,1,0:T(8,128)(2,1)}, u32[]{:S(2)}) copy-start(bf16[16,8,1664]{2,1,0:T(8,128)(2,1)} %param.14) | copy-start | bytes 1277956
  148.4 8.6 %copy-start.11 = (s32[1,1,128,1]{2,3,1,0:T(1,128)S(1)}, s32[1,1,128,1]{2,3,1,0:T(1,128)}, u32[]{:S(2)}) copy-start(s32[1,1,128,1]{2,3,1,0:T(1,128)} %param.16) | copy-start | bytes 1540
